TPU v7x, 32 devices: a whole 2x2x4 slice. The times are simulated.
32 devices in a mesh: row: 2 (over y), blk: 16 (over z, x, core).
Axes of the slice: x: 2, y: 2, z: 4, core: 2. Of those that a mesh axis runs over, the one named last changes fastest.
Arguments:
- coarse_cluster_means: bfloat16 [32768, 1024], P('blk', 'row'), may hold values from -16 to 16
- fine_cluster_means: bfloat16 [4096, 1024], P(('blk', 'row')), may hold values from -6 to 6
- block_panel_candidates: int32 [256, 8], P(('blk', 'row')), may hold values from 0 to 15, all different within a row; in each aligned block of 8 rows (0 to 7, 8 to 15, ...) at most 8 rows name the same one
- softmax_heat: float32 [1], replicated, may hold values from 0.5 to 1
Outputs:
- revised_centroids: bfloat16 [4096, 1024], P(('blk', 'row'))
- log_norm: float32 [32768], P(('blk', 'row'))
Inputs may be any that keep to these rules, and one draw needn't show every extreme that they name: `block_panel_candidates`: each row names 8 different panels; within the rows of one device no panel is named by more than 8 rows, and in some device one panel is named by exactly 8 rows.
All inputs are finite; a program needn't handle non-finite values.
Results may differ from a plain program's by a relative error of at most 0.013.
Values may be sent and summed in bfloat16 or wider, within the bound.
A program may use at most 128 MiB of HBM per device.

v0:
```python
import math

import jax
import jax.numpy as jnp
from jax import lax
from jax.sharding import PartitionSpec as P


def passed_along(shard, axis, by):
    peers = lax.axis_size(axis)
    return lax.ppermute(shard, axis, [(i, (i + by) % peers) for i in range(peers)])


def shards(coarse_cluster_means, fine_cluster_means, block_panel_candidates, softmax_heat):
    points = lax.all_to_all(coarse_cluster_means, "row", split_axis=0, concat_axis=1, tiled=True)
    rows_dev, vector_dimension = points.shape
    block_count, pair_count = block_panel_candidates.shape
    block_rows = rows_dev // block_count
    panel_rows = fine_cluster_means.shape[0]
    panels = lax.axis_size("blk")
    here = lax.axis_index("blk")
    slots = max(2, min(block_count, 2 * block_count * pair_count // panels))
    normalizing_multiplier = 1.0 / (softmax_heat[0] * math.sqrt(vector_dimension))
    blocks = points.reshape(block_count, block_rows, vector_dimension)
    block_ids = jnp.arange(block_count, dtype=jnp.int32)
    slot_ids = jnp.arange(slots, dtype=jnp.int32)

    def pick(owner):
        hits = jnp.any(block_panel_candidates == owner, axis=1)
        order = jnp.cumsum(hits.astype(jnp.int32)) - 1
        table = (order[None, :] == slot_ids[:, None]) & hits[None, :]
        index = jnp.sum(jnp.where(table, block_ids[None, :], 0), axis=1)
        valid = jnp.any(table, axis=1)
        chosen = jnp.take(blocks, index, axis=0).reshape(slots * block_rows, vector_dimension)
        return (hits, table, index, valid, chosen)

    def scores(chosen, panel):
        sqnorm = jnp.sum(jnp.square(panel.astype(jnp.float32)), axis=1)
        dots = jnp.einsum("rd,pd->rp", chosen, panel, preferred_element_type=jnp.float32)
        logit = (2.0 * dots - sqnorm[None, :]) * normalizing_multiplier
        return logit.reshape(slots, block_rows, panel_rows)

    def scout(state, panel, step):
        run_max, run_sum = state
        owner = (here - step) % panels
        hits, table, index, valid, chosen = pick(owner)
        logit = scores(chosen, panel)
        top = jnp.max(logit, axis=2)
        total = jnp.sum(jnp.exp(logit - top[:, :, None]), axis=2)
        spread = table.astype(jnp.float32)[:, :, None]
        top_back = jnp.sum(spread * top[:, None, :], axis=0)
        total_back = jnp.sum(spread * total[:, None, :], axis=0)
        newer = jnp.maximum(run_max, top_back)
        merged = run_sum * jnp.exp(run_max - newer) + total_back * jnp.exp(top_back - newer)
        chosen_rows = hits[:, None]
        return (jnp.where(chosen_rows, newer, run_max), jnp.where(chosen_rows, merged, run_sum))

    stash = jnp.zeros((1,), fine_cluster_means.dtype)
    start = (
        jnp.full((block_count, block_rows), -1e30, jnp.float32),
        jnp.zeros((block_count, block_rows), jnp.float32),
    )
    state = scout(start, fine_cluster_means, 0)

    def scout_turn(step, carry):
        panel, state, stash = carry
        panel = passed_along(panel, "blk", 1)
        return (panel, scout(state, panel, step), stash)

    outcome = lax.fori_loop(1, panels, scout_turn, (fine_cluster_means, state, stash))
    run_max, run_sum = outcome[1]
    stash = outcome[2]
    log_norm = run_max + jnp.log(run_sum)

    def weighted(panel, step):
        owner = (here - step) % panels
        hits, table, index, valid, chosen = pick(owner)
        logit = scores(chosen, panel)
        norm_rows = jnp.take(log_norm, index, axis=0)
        assign_weight = jnp.exp(logit - norm_rows[:, :, None])
        assign_weight = jnp.where(valid[:, None, None], assign_weight, 0.0).astype(jnp.bfloat16)
        flat = assign_weight.reshape(slots * block_rows, panel_rows)
        sums = lax.dot_general(
            flat, chosen, (((0,), (0,)), ((), ())), preferred_element_type=jnp.float32
        )
        mass = jnp.sum(flat.astype(jnp.float32), axis=0)
        return (sums, mass)

    def next_panel(panel):
        return passed_along(panel, "blk", 1)

    def add_sums(totals, added):
        moved = passed_along(totals, "blk", 1)
        return (moved[0] + added[0], moved[1] + added[1])

    totals = weighted(fine_cluster_means, 0)

    def sum_turn(step, carry):
        panel, totals = carry
        panel = next_panel(panel)
        return (panel, add_sums(totals, weighted(panel, step)))

    totals = lax.fori_loop(1, panels, sum_turn, (fine_cluster_means, totals))[1]
    sums, mass = passed_along((totals[0], totals[1]), "blk", 1)
    updated = ((sums + fine_cluster_means.astype(jnp.float32)) / (mass[:, None] + 1.0)).astype(
        jnp.bfloat16
    )
    return (updated, log_norm.reshape(rows_dev))


def solution(mesh):
    return jax.shard_map(
        shards,
        mesh=mesh,
        in_specs=(P("blk", "row"), P(("blk", "row"), None), P(("blk", "row"), None), P()),
        out_specs=(P(("blk", "row"), None), P(("blk", "row"))),
        check_vma=False,
    )
```

profile of v0, /device:TPU:0, one launch (start us, length us, event | category | flops | bytes accessed | tf_op | source)
XLA Modules:
  0.0 468.2 jit_solution(15076371046652590347)
XLA Ops:
  0.7 4.4 all-to-all-start
  7.3 23.6 %all-to-all-done = bf16[2,1024,512]{2,1,0:T(8,128)(2,1)S(1)} async-done(((bf16[2,1024,512]{2,1,0:T(8,128)(2,1)}), bf16[2,1024,512]{2,1,0:T(8,128)(2,1)S(1)}, u32[]{:S(2)}, u32[]{:S(2)}) %all-to-all-start) | async-done | bytes 2097184 | tf_op jit(solution)/shard_map/all_to_all | solution.py:15
  30.9 3.5 copy.29
  34.4 3.2 reshape.384
  44.2 147.4 %while.42 = (s32[]{:T(128)}, bf16[128,1024]{1,0:T(8,128)(2,1)S(1)}, f32[8,128]{1,0:T(8,128)S(1)}, f32[8,128]{1,0:T(8,128)S(1)}, s32[]{:T(128)}, /*index=5*/s32[8...) while((s32[]{:T(128)}, bf16[128,1024]{1,0:T(8,128)(2,1)S(1)}, ...), condition=%wide.region_18.20_spmd.clone.clone, body=%wide.region_9.19_spmd.clone.clone.sunk | while | flops 270702144 | bytes 13691386 | solution.py:70
  48.6 4.1 collective-permute-done
  58.4 4.1 collective-permute-done
  68.2 4.1 collective-permute-done
  78.0 4.1 collective-permute-done
  87.9 4.1 collective-permute-done
  97.7 4.1 collective-permute-done
  107.5 4.1 collective-permute-done
  117.3 4.1 collective-permute-done
  127.2 4.1 collective-permute-done
  137.0 4.1 collective-permute-done
  146.8 4.1 collective-permute-done
  156.7 4.1 collective-permute-done
  166.5 4.1 collective-permute-done
  176.3 4.1 collective-permute-done
  186.1 4.1 collective-permute-done
  192.8 2.9 convolution_bitcast_fusion.1
  195.7 259.1 %while.43 = (s32[]{:T(128)}, bf16[128,1024]{1,0:T(8,128)(2,1)}, f32[128,1024]{1,0:T(8,128)}, f32[128]{0:T(128)S(1)}, s32[]{:T(128)}, /*index=5*/s32[8,8]{1,0:T(8...) while((s32[]{:T(128)}, bf16[128,1024]{1,0:T(8,128)(2,1)}, ...), condition=%wide.region_27.30_spmd.clone.clone, body=%wide.region_20.0_spmd.clone.clone.sunk | while | flops 539889216 | bytes 28356780 | solution.py:103
  201.0 3.4 collective-permute-done.1
  208.0 2.1 collective-permute-done.3
  210.1 2.9 fusion.80
  218.3 3.4 collective-permute-done.1
  227.4 2.9 fusion.80
  235.6 3.4 collective-permute-done.1
  242.6 2.1 collective-permute-done.3
  244.7 2.9 fusion.80
  252.9 3.4 collective-permute-done.1
  261.9 2.9 fusion.80
  270.1 3.4 collective-permute-done.1
  277.1 2.1 collective-permute-done.3
  279.2 2.9 fusion.80
  287.4 3.4 collective-permute-done.1
  294.4 2.1 collective-permute-done.3
  296.5 2.9 fusion.80
  304.7 3.4 collective-permute-done.1
  311.7 2.1 collective-permute-done.3
  313.8 2.9 fusion.80
  322.0 3.4 collective-permute-done.1
  329.0 2.1 collective-permute-done.3
  331.0 2.9 fusion.80
  339.2 3.4 collective-permute-done.1
  348.3 2.9 fusion.80
  356.5 3.4 collective-permute-done.1
  363.5 2.1 collective-permute-done.3
  365.6 2.9 fusion.80
  373.8 3.4 collective-permute-done.1
  382.9 2.9 fusion.80
  391.1 3.4 collective-permute-done.1
  398.1 2.1 collective-permute-done.3
  400.1 2.9 fusion.80
  408.3 3.4 collective-permute-done.1
  415.4 2.1 collective-permute-done.3
  417.4 2.9 fusion.80
  425.6 3.4 collective-permute-done.1
  432.6 2.1 collective-permute-done.3
  434.7 2.9 fusion.80
  442.9 3.4 collective-permute-done.1
  449.9 2.1 collective-permute-done.3
  452.0 2.9 fusion.80
  454.9 11.6 %collective-permute-done.5 = f32[128]{0:T(128)S(1)} collective-permute-done((f32[128]{0:T(128)S(1)}, f32[128]{0:T(128)S(1)}, u32[]{:S(2)}, u32[]{:S(2)}) %collective-permute-start.5) | collective-permute-done | bytes 544 | tf_op jit(solution)/shard_map/ppermute | solution.py:11
  (702 shorter events, 236.1 us)
Async XLA Ops:
  0.7 30.2 %all-to-all-start = ((bf16[2,1024,512]{2,1,0:T(8,128)(2,1)}), bf16[2,1024,512]{2,1,0:T(8,128)(2,1)S(1)}, u32[]{:S(2)}, u32[]{:S(2)}) async-start(bf16[2,1024,512]{2,1,0:T(8,128)(2,1)} %bitcast.88), calls=%async_computation | async-start | bytes 4194304 | tf_op jit(solution)/shard_map/all_to_all | solution.py:15
  44.2 8.5 %collective-permute-start = (bf16[128,1024]{1,0:T(8,128)(2,1)S(1)}, bf16[128,1024]{1,0:T(8,128)(2,1)S(1)}, u32[]{:S(2)}, u32[]{:S(2)}) collective-permute-start(bf16[128,1024]{1,0:T(8,128)(2,1)S(1)} %get-tuple-element.870), channel_id=1, source_target_pairs={{0,1},{1,2},{2,3},{3,4},{4,5},{5,6},{6,7},{7,8},{8,9},{9,10},{10,1... | collective-permute-start | bytes 786440 | tf_op jit(solution)/shard_map/while/body/eval_jaxpr/ppermute | solution.py:11
  54.0 8.5 %collective-permute-start = (bf16[128,1024]{1,0:T(8,128)(2,1)S(1)}, bf16[128,1024]{1,0:T(8,128)(2,1)S(1)}, u32[]{:S(2)}, u32[]{:S(2)}) collective-permute-start(bf16[128,1024]{1,0:T(8,128)(2,1)S(1)} %get-tuple-element.870), channel_id=1, source_target_pairs={{0,1},{1,2},{2,3},{3,4},{4,5},{5,6},{6,7},{7,8},{8,9},{9,10},{10,1... | collective-permute-start | bytes 786440 | tf_op jit(solution)/shard_map/while/body/eval_jaxpr/ppermute | solution.py:11
  63.8 8.5 %collective-permute-start = (bf16[128,1024]{1,0:T(8,128)(2,1)S(1)}, bf16[128,1024]{1,0:T(8,128)(2,1)S(1)}, u32[]{:S(2)}, u32[]{:S(2)}) collective-permute-start(bf16[128,1024]{1,0:T(8,128)(2,1)S(1)} %get-tuple-element.870), channel_id=1, source_target_pairs={{0,1},{1,2},{2,3},{3,4},{4,5},{5,6},{6,7},{7,8},{8,9},{9,10},{10,1... | collective-permute-start | bytes 786440 | tf_op jit(solution)/shard_map/while/body/eval_jaxpr/ppermute | solution.py:11
  73.6 8.5 %collective-permute-start = (bf16[128,1024]{1,0:T(8,128)(2,1)S(1)}, bf16[128,1024]{1,0:T(8,128)(2,1)S(1)}, u32[]{:S(2)}, u32[]{:S(2)}) collective-permute-start(bf16[128,1024]{1,0:T(8,128)(2,1)S(1)} %get-tuple-element.870), channel_id=1, source_target_pairs={{0,1},{1,2},{2,3},{3,4},{4,5},{5,6},{6,7},{7,8},{8,9},{9,10},{10,1... | collective-permute-start | bytes 786440 | tf_op jit(solution)/shard_map/while/body/eval_jaxpr/ppermute | solution.py:11
  83.5 8.5 %collective-permute-start = (bf16[128,1024]{1,0:T(8,128)(2,1)S(1)}, bf16[128,1024]{1,0:T(8,128)(2,1)S(1)}, u32[]{:S(2)}, u32[]{:S(2)}) collective-permute-start(bf16[128,1024]{1,0:T(8,128)(2,1)S(1)} %get-tuple-element.870), channel_id=1, source_target_pairs={{0,1},{1,2},{2,3},{3,4},{4,5},{5,6},{6,7},{7,8},{8,9},{9,10},{10,1... | collective-permute-start | bytes 786440 | tf_op jit(solution)/shard_map/while/body/eval_jaxpr/ppermute | solution.py:11
  93.3 8.5 %collective-permute-start = (bf16[128,1024]{1,0:T(8,128)(2,1)S(1)}, bf16[128,1024]{1,0:T(8,128)(2,1)S(1)}, u32[]{:S(2)}, u32[]{:S(2)}) collective-permute-start(bf16[128,1024]{1,0:T(8,128)(2,1)S(1)} %get-tuple-element.870), channel_id=1, source_target_pairs={{0,1},{1,2},{2,3},{3,4},{4,5},{5,6},{6,7},{7,8},{8,9},{9,10},{10,1... | collective-permute-start | bytes 786440 | tf_op jit(solution)/shard_map/while/body/eval_jaxpr/ppermute | solution.py:11
  103.1 8.5 %collective-permute-start = (bf16[128,1024]{1,0:T(8,128)(2,1)S(1)}, bf16[128,1024]{1,0:T(8,128)(2,1)S(1)}, u32[]{:S(2)}, u32[]{:S(2)}) collective-permute-start(bf16[128,1024]{1,0:T(8,128)(2,1)S(1)} %get-tuple-element.870), channel_id=1, source_target_pairs={{0,1},{1,2},{2,3},{3,4},{4,5},{5,6},{6,7},{7,8},{8,9},{9,10},{10,1... | collective-permute-start | bytes 786440 | tf_op jit(solution)/shard_map/while/body/eval_jaxpr/ppermute | solution.py:11
  112.9 8.5 %collective-permute-start = (bf16[128,1024]{1,0:T(8,128)(2,1)S(1)}, bf16[128,1024]{1,0:T(8,128)(2,1)S(1)}, u32[]{:S(2)}, u32[]{:S(2)}) collective-permute-start(bf16[128,1024]{1,0:T(8,128)(2,1)S(1)} %get-tuple-element.870), channel_id=1, source_target_pairs={{0,1},{1,2},{2,3},{3,4},{4,5},{5,6},{6,7},{7,8},{8,9},{9,10},{10,1... | collective-permute-start | bytes 786440 | tf_op jit(solution)/shard_map/while/body/eval_jaxpr/ppermute | solution.py:11
  122.8 8.5 %collective-permute-start = (bf16[128,1024]{1,0:T(8,128)(2,1)S(1)}, bf16[128,1024]{1,0:T(8,128)(2,1)S(1)}, u32[]{:S(2)}, u32[]{:S(2)}) collective-permute-start(bf16[128,1024]{1,0:T(8,128)(2,1)S(1)} %get-tuple-element.870), channel_id=1, source_target_pairs={{0,1},{1,2},{2,3},{3,4},{4,5},{5,6},{6,7},{7,8},{8,9},{9,10},{10,1... | collective-permute-start | bytes 786440 | tf_op jit(solution)/shard_map/while/body/eval_jaxpr/ppermute | solution.py:11
  132.6 8.5 %collective-permute-start = (bf16[128,1024]{1,0:T(8,128)(2,1)S(1)}, bf16[128,1024]{1,0:T(8,128)(2,1)S(1)}, u32[]{:S(2)}, u32[]{:S(2)}) collective-permute-start(bf16[128,1024]{1,0:T(8,128)(2,1)S(1)} %get-tuple-element.870), channel_id=1, source_target_pairs={{0,1},{1,2},{2,3},{3,4},{4,5},{5,6},{6,7},{7,8},{8,9},{9,10},{10,1... | collective-permute-start | bytes 786440 | tf_op jit(solution)/shard_map/while/body/eval_jaxpr/ppermute | solution.py:11
  142.4 8.5 %collective-permute-start = (bf16[128,1024]{1,0:T(8,128)(2,1)S(1)}, bf16[128,1024]{1,0:T(8,128)(2,1)S(1)}, u32[]{:S(2)}, u32[]{:S(2)}) collective-permute-start(bf16[128,1024]{1,0:T(8,128)(2,1)S(1)} %get-tuple-element.870), channel_id=1, source_target_pairs={{0,1},{1,2},{2,3},{3,4},{4,5},{5,6},{6,7},{7,8},{8,9},{9,10},{10,1... | collective-permute-start | bytes 786440 | tf_op jit(solution)/shard_map/while/body/eval_jaxpr/ppermute | solution.py:11
  152.3 8.5 %collective-permute-start = (bf16[128,1024]{1,0:T(8,128)(2,1)S(1)}, bf16[128,1024]{1,0:T(8,128)(2,1)S(1)}, u32[]{:S(2)}, u32[]{:S(2)}) collective-permute-start(bf16[128,1024]{1,0:T(8,128)(2,1)S(1)} %get-tuple-element.870), channel_id=1, source_target_pairs={{0,1},{1,2},{2,3},{3,4},{4,5},{5,6},{6,7},{7,8},{8,9},{9,10},{10,1... | collective-permute-start | bytes 786440 | tf_op jit(solution)/shard_map/while/body/eval_jaxpr/ppermute | solution.py:11
  162.1 8.5 %collective-permute-start = (bf16[128,1024]{1,0:T(8,128)(2,1)S(1)}, bf16[128,1024]{1,0:T(8,128)(2,1)S(1)}, u32[]{:S(2)}, u32[]{:S(2)}) collective-permute-start(bf16[128,1024]{1,0:T(8,128)(2,1)S(1)} %get-tuple-element.870), channel_id=1, source_target_pairs={{0,1},{1,2},{2,3},{3,4},{4,5},{5,6},{6,7},{7,8},{8,9},{9,10},{10,1... | collective-permute-start | bytes 786440 | tf_op jit(solution)/shard_map/while/body/eval_jaxpr/ppermute | solution.py:11
  171.9 8.5 %collective-permute-start = (bf16[128,1024]{1,0:T(8,128)(2,1)S(1)}, bf16[128,1024]{1,0:T(8,128)(2,1)S(1)}, u32[]{:S(2)}, u32[]{:S(2)}) collective-permute-start(bf16[128,1024]{1,0:T(8,128)(2,1)S(1)} %get-tuple-element.870), channel_id=1, source_target_pairs={{0,1},{1,2},{2,3},{3,4},{4,5},{5,6},{6,7},{7,8},{8,9},{9,10},{10,1... | collective-permute-start | bytes 786440 | tf_op jit(solution)/shard_map/while/body/eval_jaxpr/ppermute | solution.py:11
  181.7 8.5 %collective-permute-start = (bf16[128,1024]{1,0:T(8,128)(2,1)S(1)}, bf16[128,1024]{1,0:T(8,128)(2,1)S(1)}, u32[]{:S(2)}, u32[]{:S(2)}) collective-permute-start(bf16[128,1024]{1,0:T(8,128)(2,1)S(1)} %get-tuple-element.870), channel_id=1, source_target_pairs={{0,1},{1,2},{2,3},{3,4},{4,5},{5,6},{6,7},{7,8},{8,9},{9,10},{10,1... | collective-permute-start | bytes 786440 | tf_op jit(solution)/shard_map/while/body/eval_jaxpr/ppermute | solution.py:11
  195.7 8.7 %collective-permute-start.1 = (bf16[128,1024]{1,0:T(8,128)(2,1)}, bf16[128,1024]{1,0:T(8,128)(2,1)S(1)}, u32[]{:S(2)}, u32[]{:S(2)}) collective-permute-start(bf16[128,1024]{1,0:T(8,128)(2,1)} %get-tuple-element.907), channel_id=1, source_target_pairs={{0,1},{1,2},{2,3},{3,4},{4,5},{5,6},{6,7},{7,8},{8,9},{9,10},{10,1... | collective-permute-start | bytes 786440 | tf_op jit(solution)/shard_map/while/body/eval_jaxpr/ppermute | solution.py:11
  195.7 14.4 %collective-permute-start.2 = (f32[128,1024]{1,0:T(8,128)}, f32[128,1024]{1,0:T(8,128)S(1)}, u32[]{:S(2)}, u32[]{:S(2)}) collective-permute-start(f32[128,1024]{1,0:T(8,128)} %get-tuple-element.908), channel_id=1, source_target_pairs={{0,1},{1,2},{2,3},{3,4},{4,5},{5,6},{6,7},{7,8},{8,9},{9,10},{10,1... | collective-permute-start | bytes 1572872 | tf_op jit(solution)/shard_map/while/body/eval_jaxpr/ppermute | solution.py:11
  195.7 14.4 %collective-permute-start.3 = (f32[128]{0:T(128)S(1)}, f32[128]{0:T(128)S(1)}, u32[]{:S(2)}, u32[]{:S(2)}) collective-permute-start(f32[128]{0:T(128)S(1)} %get-tuple-element.909), channel_id=1, source_target_pairs={{0,1},{1,2},{2,3},{3,4},{4,5},{5,6},{6,7},{7,8},{8,9},{9,10},{10,1... | collective-permute-start | bytes 1544 | tf_op jit(solution)/shard_map/while/body/eval_jaxpr/ppermute | solution.py:11
  213.0 8.7 %collective-permute-start.1 = (bf16[128,1024]{1,0:T(8,128)(2,1)}, bf16[128,1024]{1,0:T(8,128)(2,1)S(1)}, u32[]{:S(2)}, u32[]{:S(2)}) collective-permute-start(bf16[128,1024]{1,0:T(8,128)(2,1)} %get-tuple-element.907), channel_id=1, source_target_pairs={{0,1},{1,2},{2,3},{3,4},{4,5},{5,6},{6,7},{7,8},{8,9},{9,10},{10,1... | collective-permute-start | bytes 786440 | tf_op jit(solution)/shard_map/while/body/eval_jaxpr/ppermute | solution.py:11
  213.0 14.4 %collective-permute-start.2 = (f32[128,1024]{1,0:T(8,128)}, f32[128,1024]{1,0:T(8,128)S(1)}, u32[]{:S(2)}, u32[]{:S(2)}) collective-permute-start(f32[128,1024]{1,0:T(8,128)} %get-tuple-element.908), channel_id=1, source_target_pairs={{0,1},{1,2},{2,3},{3,4},{4,5},{5,6},{6,7},{7,8},{8,9},{9,10},{10,1... | collective-permute-start | bytes 1572872 | tf_op jit(solution)/shard_map/while/body/eval_jaxpr/ppermute | solution.py:11
  213.0 14.4 %collective-permute-start.3 = (f32[128]{0:T(128)S(1)}, f32[128]{0:T(128)S(1)}, u32[]{:S(2)}, u32[]{:S(2)}) collective-permute-start(f32[128]{0:T(128)S(1)} %get-tuple-element.909), channel_id=1, source_target_pairs={{0,1},{1,2},{2,3},{3,4},{4,5},{5,6},{6,7},{7,8},{8,9},{9,10},{10,1... | collective-permute-start | bytes 1544 | tf_op jit(solution)/shard_map/while/body/eval_jaxpr/ppermute | solution.py:11
  230.3 8.7 %collective-permute-start.1 = (bf16[128,1024]{1,0:T(8,128)(2,1)}, bf16[128,1024]{1,0:T(8,128)(2,1)S(1)}, u32[]{:S(2)}, u32[]{:S(2)}) collective-permute-start(bf16[128,1024]{1,0:T(8,128)(2,1)} %get-tuple-element.907), channel_id=1, source_target_pairs={{0,1},{1,2},{2,3},{3,4},{4,5},{5,6},{6,7},{7,8},{8,9},{9,10},{10,1... | collective-permute-start | bytes 786440 | tf_op jit(solution)/shard_map/while/body/eval_jaxpr/ppermute | solution.py:11
  230.3 14.4 %collective-permute-start.2 = (f32[128,1024]{1,0:T(8,128)}, f32[128,1024]{1,0:T(8,128)S(1)}, u32[]{:S(2)}, u32[]{:S(2)}) collective-permute-start(f32[128,1024]{1,0:T(8,128)} %get-tuple-element.908), channel_id=1, source_target_pairs={{0,1},{1,2},{2,3},{3,4},{4,5},{5,6},{6,7},{7,8},{8,9},{9,10},{10,1... | collective-permute-start | bytes 1572872 | tf_op jit(solution)/shard_map/while/body/eval_jaxpr/ppermute | solution.py:11
  230.3 14.4 %collective-permute-start.3 = (f32[128]{0:T(128)S(1)}, f32[128]{0:T(128)S(1)}, u32[]{:S(2)}, u32[]{:S(2)}) collective-permute-start(f32[128]{0:T(128)S(1)} %get-tuple-element.909), channel_id=1, source_target_pairs={{0,1},{1,2},{2,3},{3,4},{4,5},{5,6},{6,7},{7,8},{8,9},{9,10},{10,1... | collective-permute-start | bytes 1544 | tf_op jit(solution)/shard_map/while/body/eval_jaxpr/ppermute | solution.py:11
  247.5 8.7 %collective-permute-start.1 = (bf16[128,1024]{1,0:T(8,128)(2,1)}, bf16[128,1024]{1,0:T(8,128)(2,1)S(1)}, u32[]{:S(2)}, u32[]{:S(2)}) collective-permute-start(bf16[128,1024]{1,0:T(8,128)(2,1)} %get-tuple-element.907), channel_id=1, source_target_pairs={{0,1},{1,2},{2,3},{3,4},{4,5},{5,6},{6,7},{7,8},{8,9},{9,10},{10,1... | collective-permute-start | bytes 786440 | tf_op jit(solution)/shard_map/while/body/eval_jaxpr/ppermute | solution.py:11
  247.6 14.4 %collective-permute-start.2 = (f32[128,1024]{1,0:T(8,128)}, f32[128,1024]{1,0:T(8,128)S(1)}, u32[]{:S(2)}, u32[]{:S(2)}) collective-permute-start(f32[128,1024]{1,0:T(8,128)} %get-tuple-element.908), channel_id=1, source_target_pairs={{0,1},{1,2},{2,3},{3,4},{4,5},{5,6},{6,7},{7,8},{8,9},{9,10},{10,1... | collective-permute-start | bytes 1572872 | tf_op jit(solution)/shard_map/while/body/eval_jaxpr/ppermute | solution.py:11
  247.6 14.4 %collective-permute-start.3 = (f32[128]{0:T(128)S(1)}, f32[128]{0:T(128)S(1)}, u32[]{:S(2)}, u32[]{:S(2)}) collective-permute-start(f32[128]{0:T(128)S(1)} %get-tuple-element.909), channel_id=1, source_target_pairs={{0,1},{1,2},{2,3},{3,4},{4,5},{5,6},{6,7},{7,8},{8,9},{9,10},{10,1... | collective-permute-start | bytes 1544 | tf_op jit(solution)/shard_map/while/body/eval_jaxpr/ppermute | solution.py:11
  264.8 8.7 %collective-permute-start.1 = (bf16[128,1024]{1,0:T(8,128)(2,1)}, bf16[128,1024]{1,0:T(8,128)(2,1)S(1)}, u32[]{:S(2)}, u32[]{:S(2)}) collective-permute-start(bf16[128,1024]{1,0:T(8,128)(2,1)} %get-tuple-element.907), channel_id=1, source_target_pairs={{0,1},{1,2},{2,3},{3,4},{4,5},{5,6},{6,7},{7,8},{8,9},{9,10},{10,1... | collective-permute-start | bytes 786440 | tf_op jit(solution)/shard_map/while/body/eval_jaxpr/ppermute | solution.py:11
  264.8 14.4 %collective-permute-start.2 = (f32[128,1024]{1,0:T(8,128)}, f32[128,1024]{1,0:T(8,128)S(1)}, u32[]{:S(2)}, u32[]{:S(2)}) collective-permute-start(f32[128,1024]{1,0:T(8,128)} %get-tuple-element.908), channel_id=1, source_target_pairs={{0,1},{1,2},{2,3},{3,4},{4,5},{5,6},{6,7},{7,8},{8,9},{9,10},{10,1... | collective-permute-start | bytes 1572872 | tf_op jit(solution)/shard_map/while/body/eval_jaxpr/ppermute | solution.py:11
  264.8 14.4 %collective-permute-start.3 = (f32[128]{0:T(128)S(1)}, f32[128]{0:T(128)S(1)}, u32[]{:S(2)}, u32[]{:S(2)}) collective-permute-start(f32[128]{0:T(128)S(1)} %get-tuple-element.909), channel_id=1, source_target_pairs={{0,1},{1,2},{2,3},{3,4},{4,5},{5,6},{6,7},{7,8},{8,9},{9,10},{10,1... | collective-permute-start | bytes 1544 | tf_op jit(solution)/shard_map/while/body/eval_jaxpr/ppermute | solution.py:11
  282.1 8.7 %collective-permute-start.1 = (bf16[128,1024]{1,0:T(8,128)(2,1)}, bf16[128,1024]{1,0:T(8,128)(2,1)S(1)}, u32[]{:S(2)}, u32[]{:S(2)}) collective-permute-start(bf16[128,1024]{1,0:T(8,128)(2,1)} %get-tuple-element.907), channel_id=1, source_target_pairs={{0,1},{1,2},{2,3},{3,4},{4,5},{5,6},{6,7},{7,8},{8,9},{9,10},{10,1... | collective-permute-start | bytes 786440 | tf_op jit(solution)/shard_map/while/body/eval_jaxpr/ppermute | solution.py:11
  282.1 14.4 %collective-permute-start.2 = (f32[128,1024]{1,0:T(8,128)}, f32[128,1024]{1,0:T(8,128)S(1)}, u32[]{:S(2)}, u32[]{:S(2)}) collective-permute-start(f32[128,1024]{1,0:T(8,128)} %get-tuple-element.908), channel_id=1, source_target_pairs={{0,1},{1,2},{2,3},{3,4},{4,5},{5,6},{6,7},{7,8},{8,9},{9,10},{10,1... | collective-permute-start | bytes 1572872 | tf_op jit(solution)/shard_map/while/body/eval_jaxpr/ppermute | solution.py:11
  282.1 14.4 %collective-permute-start.3 = (f32[128]{0:T(128)S(1)}, f32[128]{0:T(128)S(1)}, u32[]{:S(2)}, u32[]{:S(2)}) collective-permute-start(f32[128]{0:T(128)S(1)} %get-tuple-element.909), channel_id=1, source_target_pairs={{0,1},{1,2},{2,3},{3,4},{4,5},{5,6},{6,7},{7,8},{8,9},{9,10},{10,1... | collective-permute-start | bytes 1544 | tf_op jit(solution)/shard_map/while/body/eval_jaxpr/ppermute | solution.py:11
  299.4 8.7 %collective-permute-start.1 = (bf16[128,1024]{1,0:T(8,128)(2,1)}, bf16[128,1024]{1,0:T(8,128)(2,1)S(1)}, u32[]{:S(2)}, u32[]{:S(2)}) collective-permute-start(bf16[128,1024]{1,0:T(8,128)(2,1)} %get-tuple-element.907), channel_id=1, source_target_pairs={{0,1},{1,2},{2,3},{3,4},{4,5},{5,6},{6,7},{7,8},{8,9},{9,10},{10,1... | collective-permute-start | bytes 786440 | tf_op jit(solution)/shard_map/while/body/eval_jaxpr/ppermute | solution.py:11
  299.4 14.4 %collective-permute-start.2 = (f32[128,1024]{1,0:T(8,128)}, f32[128,1024]{1,0:T(8,128)S(1)}, u32[]{:S(2)}, u32[]{:S(2)}) collective-permute-start(f32[128,1024]{1,0:T(8,128)} %get-tuple-element.908), channel_id=1, source_target_pairs={{0,1},{1,2},{2,3},{3,4},{4,5},{5,6},{6,7},{7,8},{8,9},{9,10},{10,1... | collective-permute-start | bytes 1572872 | tf_op jit(solution)/shard_map/while/body/eval_jaxpr/ppermute | solution.py:11
  299.4 14.4 %collective-permute-start.3 = (f32[128]{0:T(128)S(1)}, f32[128]{0:T(128)S(1)}, u32[]{:S(2)}, u32[]{:S(2)}) collective-permute-start(f32[128]{0:T(128)S(1)} %get-tuple-element.909), channel_id=1, source_target_pairs={{0,1},{1,2},{2,3},{3,4},{4,5},{5,6},{6,7},{7,8},{8,9},{9,10},{10,1... | collective-permute-start | bytes 1544 | tf_op jit(solution)/shard_map/while/body/eval_jaxpr/ppermute | solution.py:11
  316.6 8.7 %collective-permute-start.1 = (bf16[128,1024]{1,0:T(8,128)(2,1)}, bf16[128,1024]{1,0:T(8,128)(2,1)S(1)}, u32[]{:S(2)}, u32[]{:S(2)}) collective-permute-start(bf16[128,1024]{1,0:T(8,128)(2,1)} %get-tuple-element.907), channel_id=1, source_target_pairs={{0,1},{1,2},{2,3},{3,4},{4,5},{5,6},{6,7},{7,8},{8,9},{9,10},{10,1... | collective-permute-start | bytes 786440 | tf_op jit(solution)/shard_map/while/body/eval_jaxpr/ppermute | solution.py:11
  316.7 14.4 %collective-permute-start.2 = (f32[128,1024]{1,0:T(8,128)}, f32[128,1024]{1,0:T(8,128)S(1)}, u32[]{:S(2)}, u32[]{:S(2)}) collective-permute-start(f32[128,1024]{1,0:T(8,128)} %get-tuple-element.908), channel_id=1, source_target_pairs={{0,1},{1,2},{2,3},{3,4},{4,5},{5,6},{6,7},{7,8},{8,9},{9,10},{10,1... | collective-permute-start | bytes 1572872 | tf_op jit(solution)/shard_map/while/body/eval_jaxpr/ppermute | solution.py:11
  316.7 14.4 %collective-permute-start.3 = (f32[128]{0:T(128)S(1)}, f32[128]{0:T(128)S(1)}, u32[]{:S(2)}, u32[]{:S(2)}) collective-permute-start(f32[128]{0:T(128)S(1)} %get-tuple-element.909), channel_id=1, source_target_pairs={{0,1},{1,2},{2,3},{3,4},{4,5},{5,6},{6,7},{7,8},{8,9},{9,10},{10,1... | collective-permute-start | bytes 1544 | tf_op jit(solution)/shard_map/while/body/eval_jaxpr/ppermute | solution.py:11
  333.9 8.7 %collective-permute-start.1 = (bf16[128,1024]{1,0:T(8,128)(2,1)}, bf16[128,1024]{1,0:T(8,128)(2,1)S(1)}, u32[]{:S(2)}, u32[]{:S(2)}) collective-permute-start(bf16[128,1024]{1,0:T(8,128)(2,1)} %get-tuple-element.907), channel_id=1, source_target_pairs={{0,1},{1,2},{2,3},{3,4},{4,5},{5,6},{6,7},{7,8},{8,9},{9,10},{10,1... | collective-permute-start | bytes 786440 | tf_op jit(solution)/shard_map/while/body/eval_jaxpr/ppermute | solution.py:11
  333.9 14.4 %collective-permute-start.2 = (f32[128,1024]{1,0:T(8,128)}, f32[128,1024]{1,0:T(8,128)S(1)}, u32[]{:S(2)}, u32[]{:S(2)}) collective-permute-start(f32[128,1024]{1,0:T(8,128)} %get-tuple-element.908), channel_id=1, source_target_pairs={{0,1},{1,2},{2,3},{3,4},{4,5},{5,6},{6,7},{7,8},{8,9},{9,10},{10,1... | collective-permute-start | bytes 1572872 | tf_op jit(solution)/shard_map/while/body/eval_jaxpr/ppermute | solution.py:11
  333.9 14.4 %collective-permute-start.3 = (f32[128]{0:T(128)S(1)}, f32[128]{0:T(128)S(1)}, u32[]{:S(2)}, u32[]{:S(2)}) collective-permute-start(f32[128]{0:T(128)S(1)} %get-tuple-element.909), channel_id=1, source_target_pairs={{0,1},{1,2},{2,3},{3,4},{4,5},{5,6},{6,7},{7,8},{8,9},{9,10},{10,1... | collective-permute-start | bytes 1544 | tf_op jit(solution)/shard_map/while/body/eval_jaxpr/ppermute | solution.py:11
  351.2 8.7 %collective-permute-start.1 = (bf16[128,1024]{1,0:T(8,128)(2,1)}, bf16[128,1024]{1,0:T(8,128)(2,1)S(1)}, u32[]{:S(2)}, u32[]{:S(2)}) collective-permute-start(bf16[128,1024]{1,0:T(8,128)(2,1)} %get-tuple-element.907), channel_id=1, source_target_pairs={{0,1},{1,2},{2,3},{3,4},{4,5},{5,6},{6,7},{7,8},{8,9},{9,10},{10,1... | collective-permute-start | bytes 786440 | tf_op jit(solution)/shard_map/while/body/eval_jaxpr/ppermute | solution.py:11
  351.2 14.4 %collective-permute-start.2 = (f32[128,1024]{1,0:T(8,128)}, f32[128,1024]{1,0:T(8,128)S(1)}, u32[]{:S(2)}, u32[]{:S(2)}) collective-permute-start(f32[128,1024]{1,0:T(8,128)} %get-tuple-element.908), channel_id=1, source_target_pairs={{0,1},{1,2},{2,3},{3,4},{4,5},{5,6},{6,7},{7,8},{8,9},{9,10},{10,1... | collective-permute-start | bytes 1572872 | tf_op jit(solution)/shard_map/while/body/eval_jaxpr/ppermute | solution.py:11
  351.2 14.4 %collective-permute-start.3 = (f32[128]{0:T(128)S(1)}, f32[128]{0:T(128)S(1)}, u32[]{:S(2)}, u32[]{:S(2)}) collective-permute-start(f32[128]{0:T(128)S(1)} %get-tuple-element.909), channel_id=1, source_target_pairs={{0,1},{1,2},{2,3},{3,4},{4,5},{5,6},{6,7},{7,8},{8,9},{9,10},{10,1... | collective-permute-start | bytes 1544 | tf_op jit(solution)/shard_map/while/body/eval_jaxpr/ppermute | solution.py:11
  368.5 8.7 %collective-permute-start.1 = (bf16[128,1024]{1,0:T(8,128)(2,1)}, bf16[128,1024]{1,0:T(8,128)(2,1)S(1)}, u32[]{:S(2)}, u32[]{:S(2)}) collective-permute-start(bf16[128,1024]{1,0:T(8,128)(2,1)} %get-tuple-element.907), channel_id=1, source_target_pairs={{0,1},{1,2},{2,3},{3,4},{4,5},{5,6},{6,7},{7,8},{8,9},{9,10},{10,1... | collective-permute-start | bytes 786440 | tf_op jit(solution)/shard_map/while/body/eval_jaxpr/ppermute | solution.py:11
  368.5 14.4 %collective-permute-start.2 = (f32[128,1024]{1,0:T(8,128)}, f32[128,1024]{1,0:T(8,128)S(1)}, u32[]{:S(2)}, u32[]{:S(2)}) collective-permute-start(f32[128,1024]{1,0:T(8,128)} %get-tuple-element.908), channel_id=1, source_target_pairs={{0,1},{1,2},{2,3},{3,4},{4,5},{5,6},{6,7},{7,8},{8,9},{9,10},{10,1... | collective-permute-start | bytes 1572872 | tf_op jit(solution)/shard_map/while/body/eval_jaxpr/ppermute | solution.py:11
  368.5 14.4 %collective-permute-start.3 = (f32[128]{0:T(128)S(1)}, f32[128]{0:T(128)S(1)}, u32[]{:S(2)}, u32[]{:S(2)}) collective-permute-start(f32[128]{0:T(128)S(1)} %get-tuple-element.909), channel_id=1, source_target_pairs={{0,1},{1,2},{2,3},{3,4},{4,5},{5,6},{6,7},{7,8},{8,9},{9,10},{10,1... | collective-permute-start | bytes 1544 | tf_op jit(solution)/shard_map/while/body/eval_jaxpr/ppermute | solution.py:11
  385.7 8.7 %collective-permute-start.1 = (bf16[128,1024]{1,0:T(8,128)(2,1)}, bf16[128,1024]{1,0:T(8,128)(2,1)S(1)}, u32[]{:S(2)}, u32[]{:S(2)}) collective-permute-start(bf16[128,1024]{1,0:T(8,128)(2,1)} %get-tuple-element.907), channel_id=1, source_target_pairs={{0,1},{1,2},{2,3},{3,4},{4,5},{5,6},{6,7},{7,8},{8,9},{9,10},{10,1... | collective-permute-start | bytes 786440 | tf_op jit(solution)/shard_map/while/body/eval_jaxpr/ppermute | solution.py:11
  385.8 14.4 %collective-permute-start.2 = (f32[128,1024]{1,0:T(8,128)}, f32[128,1024]{1,0:T(8,128)S(1)}, u32[]{:S(2)}, u32[]{:S(2)}) collective-permute-start(f32[128,1024]{1,0:T(8,128)} %get-tuple-element.908), channel_id=1, source_target_pairs={{0,1},{1,2},{2,3},{3,4},{4,5},{5,6},{6,7},{7,8},{8,9},{9,10},{10,1... | collective-permute-start | bytes 1572872 | tf_op jit(solution)/shard_map/while/body/eval_jaxpr/ppermute | solution.py:11
  385.8 14.4 %collective-permute-start.3 = (f32[128]{0:T(128)S(1)}, f32[128]{0:T(128)S(1)}, u32[]{:S(2)}, u32[]{:S(2)}) collective-permute-start(f32[128]{0:T(128)S(1)} %get-tuple-element.909), channel_id=1, source_target_pairs={{0,1},{1,2},{2,3},{3,4},{4,5},{5,6},{6,7},{7,8},{8,9},{9,10},{10,1... | collective-permute-start | bytes 1544 | tf_op jit(solution)/shard_map/while/body/eval_jaxpr/ppermute | solution.py:11
  403.0 8.7 %collective-permute-start.1 = (bf16[128,1024]{1,0:T(8,128)(2,1)}, bf16[128,1024]{1,0:T(8,128)(2,1)S(1)}, u32[]{:S(2)}, u32[]{:S(2)}) collective-permute-start(bf16[128,1024]{1,0:T(8,128)(2,1)} %get-tuple-element.907), channel_id=1, source_target_pairs={{0,1},{1,2},{2,3},{3,4},{4,5},{5,6},{6,7},{7,8},{8,9},{9,10},{10,1... | collective-permute-start | bytes 786440 | tf_op jit(solution)/shard_map/while/body/eval_jaxpr/ppermute | solution.py:11
  403.0 14.4 %collective-permute-start.2 = (f32[128,1024]{1,0:T(8,128)}, f32[128,1024]{1,0:T(8,128)S(1)}, u32[]{:S(2)}, u32[]{:S(2)}) collective-permute-start(f32[128,1024]{1,0:T(8,128)} %get-tuple-element.908), channel_id=1, source_target_pairs={{0,1},{1,2},{2,3},{3,4},{4,5},{5,6},{6,7},{7,8},{8,9},{9,10},{10,1... | collective-permute-start | bytes 1572872 | tf_op jit(solution)/shard_map/while/body/eval_jaxpr/ppermute | solution.py:11
  403.0 14.4 %collective-permute-start.3 = (f32[128]{0:T(128)S(1)}, f32[128]{0:T(128)S(1)}, u32[]{:S(2)}, u32[]{:S(2)}) collective-permute-start(f32[128]{0:T(128)S(1)} %get-tuple-element.909), channel_id=1, source_target_pairs={{0,1},{1,2},{2,3},{3,4},{4,5},{5,6},{6,7},{7,8},{8,9},{9,10},{10,1... | collective-permute-start | bytes 1544 | tf_op jit(solution)/shard_map/while/body/eval_jaxpr/ppermute | solution.py:11
  420.3 8.7 %collective-permute-start.1 = (bf16[128,1024]{1,0:T(8,128)(2,1)}, bf16[128,1024]{1,0:T(8,128)(2,1)S(1)}, u32[]{:S(2)}, u32[]{:S(2)}) collective-permute-start(bf16[128,1024]{1,0:T(8,128)(2,1)} %get-tuple-element.907), channel_id=1, source_target_pairs={{0,1},{1,2},{2,3},{3,4},{4,5},{5,6},{6,7},{7,8},{8,9},{9,10},{10,1... | collective-permute-start | bytes 786440 | tf_op jit(solution)/shard_map/while/body/eval_jaxpr/ppermute | solution.py:11
  420.3 14.4 %collective-permute-start.2 = (f32[128,1024]{1,0:T(8,128)}, f32[128,1024]{1,0:T(8,128)S(1)}, u32[]{:S(2)}, u32[]{:S(2)}) collective-permute-start(f32[128,1024]{1,0:T(8,128)} %get-tuple-element.908), channel_id=1, source_target_pairs={{0,1},{1,2},{2,3},{3,4},{4,5},{5,6},{6,7},{7,8},{8,9},{9,10},{10,1... | collective-permute-start | bytes 1572872 | tf_op jit(solution)/shard_map/while/body/eval_jaxpr/ppermute | solution.py:11
  420.3 14.4 %collective-permute-start.3 = (f32[128]{0:T(128)S(1)}, f32[128]{0:T(128)S(1)}, u32[]{:S(2)}, u32[]{:S(2)}) collective-permute-start(f32[128]{0:T(128)S(1)} %get-tuple-element.909), channel_id=1, source_target_pairs={{0,1},{1,2},{2,3},{3,4},{4,5},{5,6},{6,7},{7,8},{8,9},{9,10},{10,1... | collective-permute-start | bytes 1544 | tf_op jit(solution)/shard_map/while/body/eval_jaxpr/ppermute | solution.py:11
  437.6 8.7 %collective-permute-start.1 = (bf16[128,1024]{1,0:T(8,128)(2,1)}, bf16[128,1024]{1,0:T(8,128)(2,1)S(1)}, u32[]{:S(2)}, u32[]{:S(2)}) collective-permute-start(bf16[128,1024]{1,0:T(8,128)(2,1)} %get-tuple-element.907), channel_id=1, source_target_pairs={{0,1},{1,2},{2,3},{3,4},{4,5},{5,6},{6,7},{7,8},{8,9},{9,10},{10,1... | collective-permute-start | bytes 786440 | tf_op jit(solution)/shard_map/while/body/eval_jaxpr/ppermute | solution.py:11
  437.6 14.4 %collective-permute-start.2 = (f32[128,1024]{1,0:T(8,128)}, f32[128,1024]{1,0:T(8,128)S(1)}, u32[]{:S(2)}, u32[]{:S(2)}) collective-permute-start(f32[128,1024]{1,0:T(8,128)} %get-tuple-element.908), channel_id=1, source_target_pairs={{0,1},{1,2},{2,3},{3,4},{4,5},{5,6},{6,7},{7,8},{8,9},{9,10},{10,1... | collective-permute-start | bytes 1572872 | tf_op jit(solution)/shard_map/while/body/eval_jaxpr/ppermute | solution.py:11
  437.6 14.4 %collective-permute-start.3 = (f32[128]{0:T(128)S(1)}, f32[128]{0:T(128)S(1)}, u32[]{:S(2)}, u32[]{:S(2)}) collective-permute-start(f32[128]{0:T(128)S(1)} %get-tuple-element.909), channel_id=1, source_target_pairs={{0,1},{1,2},{2,3},{3,4},{4,5},{5,6},{6,7},{7,8},{8,9},{9,10},{10,1... | collective-permute-start | bytes 1544 | tf_op jit(solution)/shard_map/while/body/eval_jaxpr/ppermute | solution.py:11
  454.8 13.3 %copy-start.1 = (f32[8,128]{1,0:T(8,128)}, f32[8,128]{1,0:T(8,128)S(1)}, u32[]{:S(2)}) copy-start(f32[8,128]{1,0:T(8,128)S(1)} %get-tuple-element.936) | copy-start | bytes 12292
  454.9 11.6 %collective-permute-start.4 = (f32[128,1024]{1,0:T(8,128)}, f32[128,1024]{1,0:T(8,128)S(1)}, u32[]{:S(2)}, u32[]{:S(2)}) collective-permute-start(f32[128,1024]{1,0:T(8,128)} %get-tuple-element.550), channel_id=1, source_target_pairs={{0,1},{1,2},{2,3},{3,4},{4,5},{5,6},{6,7},{7,8},{8,9},{9,10},{10,1... | collective-permute-start | bytes 1572872 | tf_op jit(solution)/shard_map/ppermute | solution.py:11
  454.9 11.6 %collective-permute-start.5 = (f32[128]{0:T(128)S(1)}, f32[128]{0:T(128)S(1)}, u32[]{:S(2)}, u32[]{:S(2)}) collective-permute-start(f32[128]{0:T(128)S(1)} %get-tuple-element.551), channel_id=1, source_target_pairs={{0,1},{1,2},{2,3},{3,4},{4,5},{5,6},{6,7},{7,8},{8,9},{9,10},{10,1... | collective-permute-start | bytes 1544 | tf_op jit(solution)/shard_map/ppermute | solution.py:11
  (18 other events, 67.0 us)
where the time goes:
time: 471 us; the launch traced here: 468 us
  waiting for transfers between devices  179 us (38%)
  local copies, waits for them, and re-layouts  111 us (24%)
  other arithmetic  86.3 us (18%)
  matrix products  82.8 us (18%)
  starting transfers between devices  5.32 us (1%)
    ppermute x62, waiting for transfers between devices, passed_along(): lax.ppermute(shard, axis, [(i, (i + by) % peers) for i in range(peers)])  156 us
    gather x31, local copies, waits for them, and re-layouts, pick(): jnp.take(blocks, index, axis=0)  62.1 us
    select_n x62, other arithmetic, pick(): jnp.take(blocks, index, axis=0)  57.7 us
    dot_general x16, matrix products, weighted(): lax.dot_general(flat, chosen, (((0,), (0,)), ((), ())), preferred_element...  46.1 us
    dot_general x31, matrix products, scores(): jnp.einsum('rd,pd->rp', chosen, panel, preferred_element_type=jnp.float32)  36.6 us
    all_to_all x1, waiting for transfers between devices, shards(): lax.all_to_all(coarse_cluster_means, 'row', split_axis=0, concat_axis=1,...  23.6 us
    reshape x16, local copies, waits for them, and re-layouts, scores(): return logit.reshape(slots, block_rows, panel_rows)  18.7 us
    while x60, local copies, waits for them, and re-layouts  10.9 us
  transfers between devices with their start and end apart: 63, of which 47 were waited for; matrix products, arithmetic and copies ran while one was open for 42% of the time, Pallas kernels for 0%

commit v1 on v0

v1 whole, which is shorter than its diff:
```python
import math

import jax
import jax.numpy as jnp
from jax import lax
from jax.sharding import PartitionSpec as P


def shards(coarse, fine, candidates, heat):
    points = lax.all_to_all(coarse, "row", split_axis=0, concat_axis=1, tiled=True)
    panels = lax.all_gather(fine, "blk", axis=0, tiled=True)
    rows, width = points.shape
    blocks = candidates.shape[0]
    count = lax.axis_size("blk")
    scale = 1.0 / (heat[0] * math.sqrt(width))
    sqnorm = jnp.sum(jnp.square(panels.astype(jnp.float32)), axis=1)
    dots = jnp.einsum("pd,rd->pr", panels, points, preferred_element_type=jnp.float32)
    logit = (2.0 * dots - sqnorm[:, None]) * scale
    named = jnp.any(candidates[None, :, :] == jnp.arange(count)[:, None, None], axis=2)
    logit = logit.reshape(count, -1, blocks, rows // blocks)
    logit = jnp.where(named[:, None, :, None], logit, -jnp.inf).reshape(-1, rows)
    top = jnp.max(logit, axis=0)
    log_norm = top + jnp.log(jnp.sum(jnp.exp(logit - top), axis=0))
    weight = jnp.exp(logit - log_norm).astype(jnp.bfloat16)
    sums = jnp.dot(weight, points, preferred_element_type=jnp.float32)
    mass = jnp.sum(weight.astype(jnp.float32), axis=1)
    sums = lax.psum_scatter(sums, "blk", scatter_dimension=0, tiled=True)
    mass = lax.psum_scatter(mass, "blk", scatter_dimension=0, tiled=True)
    new = (sums + fine.astype(jnp.float32)) / (mass[:, None] + 1.0)
    return new.astype(jnp.bfloat16), log_norm


def solution(mesh):
    return jax.shard_map(
        shards,
        mesh=mesh,
        in_specs=(P("blk", "row"), P(("blk", "row"), None), P(("blk", "row"), None), P()),
        out_specs=(P(("blk", "row"), None), P(("blk", "row"))),
        check_vma=False,
    )
```

time: 471 us -> 198 us (0.42)
  local copies, waits for them, and re-layouts: 111 us -> 6.8 us
  other arithmetic: 86.3 us -> 11.9 us
  matrix products: 82.8 us -> 14.9 us
  waiting for transfers between devices: 179 us -> 113 us
  blocking collectives: 0 us -> 31.8 us
  between operations: 1.43 us -> 15.4 us
    ppermute x62 -> x0, waiting for transfers between devices: 156 us -> none  [passed_along(): lax.ppermute(shard, axis, [(i, (i + by) % peers) for i in range(peers)])]
    gather x47 -> x0, local copies, waits for them, and re-layouts: 71 us -> none  [the longest x31 62.1 us: pick(): jnp.take(blocks, index, axis=0)]
    dot_general x47 -> x2, matrix products: 82.8 us -> 14.9 us  [the longest x1 7.82 us: shards(): jnp.einsum('pd,rd->pr', panels, points, preferred_element_type=jnp.float32)]
    reduce_scatter x0 -> x1, waiting for transfers between devices: none -> 64.7 us  [shards(): sums = lax.psum_scatter(sums, 'blk', scatter_dimension=0, tiled=True)]
    select_n x94 -> x0, other arithmetic: 59.9 us -> none  [the longest x62 57.7 us: pick(): jnp.take(blocks, index, axis=0)]
    unnamed x0 -> x1, blocking collectives: none -> 31.8 us
    reshape x18 -> x0, local copies, waits for them, and re-layouts: 25.5 us -> none  [the longest x16 18.7 us: scores(): return logit.reshape(slots, block_rows, panel_rows)]
    all_gather x0 -> x1, waiting for transfers between devices: none -> 22.9 us  [shards(): panels = lax.all_gather(fine, 'blk', axis=0, tiled=True)]
  transfers between devices with their start and end apart: 63 -> 3, of which waited for: 47 -> 3; matrix products, arithmetic and copies ran while one was open for 42% -> 5% of each run, Pallas kernels for 0% -> 0%
where the time goes in v1:
time: 198 us
  waiting for transfers between devices  113 us (57%)
  blocking collectives  31.8 us (16%)
  between operations  15.4 us (8%)
  matrix products  14.9 us (8%)
  other arithmetic  11.9 us (6%)
  local copies, waits for them, and re-layouts  6.8 us (3%)
  starting transfers between devices  4.29 us (2%)
    reduce_scatter x1, waiting for transfers between devices, shards(): sums = lax.psum_scatter(sums, 'blk', scatter_dimension=0, tiled=True)  64.7 us
    unnamed x1, blocking collectives  31.8 us
    all_to_all x1, waiting for transfers between devices, shards(): lax.all_to_all(coarse, 'row', split_axis=0, concat_axis=1, tiled=True)  24.3 us
    all_gather x1, waiting for transfers between devices, shards(): panels = lax.all_gather(fine, 'blk', axis=0, tiled=True)  22.9 us
    dot_general x1, matrix products, shards(): jnp.einsum('pd,rd->pr', panels, points, preferred_element_type=jnp.float32)  7.82 us
    dot_general x1, matrix products, shards(): sums = jnp.dot(weight, points, preferred_element_type=jnp.float32)  7.11 us
    reduce_sum x1, other arithmetic, shards(): mass = jnp.sum(weight.astype(jnp.float32), axis=1)  4.92 us
    all_to_all x1, starting transfers between devices, shards(): lax.all_to_all(coarse, 'row', split_axis=0, concat_axis=1, tiled=True)  4.25 us
  transfers between devices with their start and end apart: 3, of which 3 were waited for; matrix products, arithmetic and copies ran while one was open for 5% of the time, Pallas kernels for 0%

profile of v1, /device:TPU:0, one launch (start us, length us, event | category | flops | bytes accessed | tf_op | source)
XLA Modules:
  0.0 197.7 jit_solution(16069988022416714529)
XLA Ops:
  7.2 0.0 all-gather.2.cloned.1.call-start
  7.2 0.7 all-gather.2.cloned.1.call-update
  7.9 4.2 %all-to-all-start = ((bf16[2,1024,512]{2,1,0:T(8,128)(2,1)}), bf16[2,1024,512]{2,1,0:T(8,128)(2,1)S(1)}, u32[]{:S(2)}, u32[]{:S(2)}) async-start(bf16[2,1024,512]{2,1,0:T(8,128)(2,1)} %bitcast.14), calls=%async_computation | async-start | bytes 4194304 | tf_op jit(solution)/shard_map/all_to_all | solution.py:10
  12.1 0.0 reduce-scatter.2.cloned.1.call-start
  12.1 0.8 fusion.1
  12.9 0.1 copy.8
  13.7 24.3 %all-to-all-done = bf16[2,1024,512]{2,1,0:T(8,128)(2,1)S(1)} async-done(((bf16[2,1024,512]{2,1,0:T(8,128)(2,1)}), bf16[2,1024,512]{2,1,0:T(8,128)(2,1)S(1)}, u32[]{:S(2)}, u32[]{:S(2)}) %all-to-all-start) | async-done | bytes 2097184 | tf_op jit(solution)/shard_map/all_to_all | solution.py:10
  38.0 2.5 %copy.9 = bf16[1024,2,512]{0,2,1:T(8,128)(2,1)} copy(bf16[1024,2,512]{2,0,1:T(8,128)(2,1)S(1)} %bitcast.12) | data formatting | bytes 4194304 | tf_op jit(solution)/shard_map/all_to_all | solution.py:10
  40.5 22.9 %all-gather.2.cloned.1.call-done = bf16[2048,1024]{1,0:T(8,128)(2,1)} async-done(((bf16[128,1024]{1,0:T(8,128)(2,1)}), bf16[2048,1024]{1,0:T(8,128)(2,1)}) %all-gather.2.cloned.1.call-update) | async-done | bytes 4194320 | tf_op jit(solution)/shard_map/all_gather | solution.py:11
  63.5 3.1 %multiply_reduce_fusion = f32[2048]{0:T(1024)S(1)} fusion(bf16[2048,1024]{1,0:T(8,128)(2,1)} %all-gather.2.cloned.1.call-done), kind=kLoop, calls=%fused_computation.4 | loop fusion | flops 6289408 | bytes 4202496 | tf_op jit(solution)/shard_map/reduce_sum | solution.py:16
  66.5 0.6 broadcast_in_dim.14
  67.1 7.8 %fusion.2 = (f32[1024]{0:T(1024)S(1)}, f32[2048,1024]{1,0:T(8,128)S(1)}) fusion(f32[]{:T(128)} %bitcast.3, f32[2048]{0:T(1024)S(1)} %multiply_reduce_fusion, bf16[2048,1024]{1,0:T(8,128)(2,1)} %all-gather.2.cloned.1.call-done, bf16[1024,1024]{0,1:T(8,128)(2,1)} %bitcast.15, pred[256,8,8,128]{3,2,1,0:T(8,128)(4,1)S(1)} %bitcast.13), kind=kOutput, calls=%fused_computation.11 | convolution fusion | flops 4305452032 | bytes 16789508 | tf_op jit(solution)/shard_map/pd,rd->pr/dot_general | solution.py:17
  75.0 0.0 copy-start
  75.0 0.0 copy-start.1
  75.0 1.2 exponential_reduce_fusion
  76.2 2.3 %copy-done = f32[2048,1024]{1,0:T(8,128)} copy-done((f32[2048,1024]{1,0:T(8,128)}, f32[2048,1024]{1,0:T(8,128)S(1)}, u32[]{:S(2)}) %copy-start) | copy-done | bytes 8388632
  78.5 0.0 copy-done.1
  78.5 0.0 copy-start.3
  78.5 7.1 %fusion = f32[2048,1024]{1,0:T(8,128)} fusion(bf16[1024,1024]{0,1:T(8,128)(2,1)S(1)} %bitcast.16, f32[2048,1024]{1,0:T(8,128)S(1)} %get-tuple-element.3, f32[1024]{0:T(1024)S(1)} %log_add_fusion), kind=kOutput, calls=%fused_computation.5 | convolution fusion | flops 4299161600 | bytes 18878464 | tf_op jit(solution)/shard_map/dot_general | solution.py:25
  85.6 0.0 copy-start.4
  85.6 0.0 copy-start.2
  85.6 0.0 reduce-scatter.2.cloned.1.call-update
  85.7 0.6 copy-done.4
  86.3 0.6 dynamic-slice
  87.5 0.0 copy-done.3
  87.5 4.9 %convert_reduce_fusion = f32[2048]{0:T(1024)S(1)} fusion(f32[2048,1024]{1,0:T(8,128)} %copy-done, f32[1024]{0:T(1024)S(1)} %log_add_fusion), kind=kLoop, calls=%fused_computation | loop fusion | flops 8386560 | bytes 8400896 | tf_op jit(solution)/shard_map/reduce_sum | solution.py:26
  92.5 31.8 %all-reduce = f32[2048]{0:T(1024)S(1)} all-reduce(f32[2048]{0:T(1024)S(1)} %convert_reduce_fusion), channel_id=3, replica_groups=mesh['row'=2,'blk'=16] {'blk'}, use_global_device_ids=true, to_apply=%region_6.7.clone | all-reduce | flops 2048 | bytes 16384
  124.2 0.1 dynamic-slice_add_fusion
  124.3 64.7 %reduce-scatter.2.cloned.1.call-done = f32[128,1024]{1,0:T(8,128)} async-done(((f32[2048,1024]{1,0:T(8,128)}), f32[128,1024]{1,0:T(8,128)}) %reduce-scatter.2.cloned.1.call-update) | async-done | bytes 524304 | tf_op jit(solution)/shard_map/reduce_scatter | solution.py:27
  189.0 0.0 copy-done.2
  189.0 1.9 divide_convert_fusion
  (1 shorter events, 0.0 us)
Async XLA Ops:
  7.2 56.3 %all-gather.2.cloned.1.call-start = ((), (), s32[]{:S(2)}) async-start(), calls=%async_computation.2 | async-start | bytes 4456448 | tf_op jit(solution)/shard_map/all_gather | solution.py:11
  7.9 30.1 %all-to-all-start = ((bf16[2,1024,512]{2,1,0:T(8,128)(2,1)}), bf16[2,1024,512]{2,1,0:T(8,128)(2,1)S(1)}, u32[]{:S(2)}, u32[]{:S(2)}) async-start(bf16[2,1024,512]{2,1,0:T(8,128)(2,1)} %bitcast.14), calls=%async_computation | async-start | bytes 4194304 | tf_op jit(solution)/shard_map/all_to_all | solution.py:10
  12.1 176.9 %reduce-scatter.2.cloned.1.call-start = ((), (), s32[]{:S(2)}) async-start(), calls=%async_computation.3 | async-start | bytes 8912896 | tf_op jit(solution)/shard_map/reduce_scatter | solution.py:27
  75.0 3.5 %copy-start = (f32[2048,1024]{1,0:T(8,128)}, f32[2048,1024]{1,0:T(8,128)S(1)}, u32[]{:S(2)}) copy-start(f32[2048,1024]{1,0:T(8,128)S(1)} %get-tuple-element.3) | copy-start | bytes 25165828
  75.0 3.5 %copy-start.1 = (bf16[1024,2,512]{0,2,1:T(8,128)(2,1)S(1)}, bf16[1024,2,512]{0,2,1:T(8,128)(2,1)}, u32[]{:S(2)}) copy-start(bf16[1024,2,512]{0,2,1:T(8,128)(2,1)} %copy.9) | copy-start | bytes 6291460
  78.5 9.0 %copy-start.3 = (f32[1024]{0:T(1024)}, f32[1024]{0:T(1024)S(1)}, u32[]{:S(2)}) copy-start(f32[1024]{0:T(1024)S(1)} %log_add_fusion) | copy-start | bytes 12292
  85.6 0.7 copy-start.4
  85.6 103.4 %copy-start.2 = (bf16[128,1024]{1,0:T(8,128)(2,1)S(1)}, bf16[128,1024]{1,0:T(8,128)(2,1)}, u32[]{:S(2)}) copy-start(bf16[128,1024]{1,0:T(8,128)(2,1)} %param.5) | copy-start | bytes 786436
Sparse Core Ops, SparseCore 0:
  10.2 53.2 all-gather.1
  85.8 103.1 reduce-scatter.1

commit v2 on v1

v2 whole, which is shorter than its diff:
```python
import functools
import math

import jax
import jax.numpy as jnp
from jax import lax
from jax.experimental import pallas as pl
from jax.experimental.pallas import tpu as pltpu
from jax.sharding import PartitionSpec as P

MESH = pl.DeviceIdType.MESH
F32 = jnp.float32
BF16 = jnp.bfloat16
LANES = 256


def kernel(
    dims, n_row, x_ref, fine_ref, bias_ref, heat_ref, out_ref, lse_ref,
    xbuf, panels, logits, norms, top, total, weights, part, in_c, send_b, in_b, send_a, in_a,
    mass_out, mass_in,
    x_send, x_recv, g_send, g_recv, c_send, c_recv, b_send, b_recv, a_send, a_recv, m_send, m_recv,
    own_sem,
):
    d0, d1, d2 = dims
    n_blk = d0 * d1 * d2
    row = lax.axis_index("row")
    blk = lax.axis_index("blk")
    i2 = lax.rem(blk, d2)
    i1 = lax.rem(lax.div(blk, d2), d1)
    i0 = lax.div(blk, d1 * d2)
    size = fine_ref.shape[0]
    width = fine_ref.shape[1]
    rows = xbuf.shape[1]
    feats = xbuf.shape[2]
    pair = d2 * size
    chunks = x_send.shape[1]
    step = rows // chunks

    def at(o0, o1, o2, sign):
        a = lax.rem(i0 + sign * o0 + d0, d0)
        b = lax.rem(i1 + sign * o1 + d1, d1)
        c = lax.rem(i2 + sign * o2 + d2, d2)
        return (a * d1 + b) * d2 + c

    def panel(owner, ref):
        return ref.at[pl.ds(pl.multiple_of(owner * size, size), size), :]

    def base_of(o0, o1, sign):
        a = lax.rem(i0 + sign * o0 + d0, d0)
        b = lax.rem(i1 + sign * o1 + d1, d1)
        return (a * d1 + b) * d2

    def remote(src, dst, send, recv, to):
        copy = pltpu.make_async_remote_copy(
            src_ref=src, dst_ref=dst, send_sem=send, recv_sem=recv,
            device_id=to, device_id_type=MESH,
        )
        copy.start()
        return copy

    barrier = pltpu.get_barrier_semaphore()
    for d in range(1, n_row):
        pl.semaphore_signal(
            barrier, inc=1, device_id={"row": lax.rem(row + d, n_row)}, device_id_type=MESH
        )
    for d in range(1, n_blk):
        pl.semaphore_signal(
            barrier, inc=1, device_id={"blk": lax.rem(blk + d, n_blk)}, device_id_type=MESH
        )
    own_x = pltpu.make_async_copy(
        x_ref.at[pl.ds(pl.multiple_of(row * rows, rows), rows), :], xbuf.at[row], own_sem.at[0]
    )
    own_x.start()
    own_panel = pltpu.make_async_copy(fine_ref, panel(blk, panels), own_sem.at[1])
    own_panel.start()
    pl.semaphore_wait(barrier, n_row - 1 + n_blk - 1)

    gathered = {}

    def gather(o, axis, hop):
        final = list(o)
        final[axis] = hop
        final = tuple(final)
        move = [0, 0, 0]
        move[axis] = hop
        owner = at(*o, -1)
        src = fine_ref if o == (0, 0, 0) else panel(owner, panels)
        gathered[final] = remote(
            src, panel(owner, panels), g_send.at[final], g_recv.at[final],
            {"blk": at(*move, 1)},
        )

    for o1 in range(1, d1):
        gather((0, 0, 0), 1, o1)
    for o0 in range(1, d0):
        gather((0, 0, 0), 0, o0)
    for o2 in range(1, d2):
        gather((0, 0, 0), 2, o2)
    points = []
    for c in range(chunks):
        for d in range(1, n_row):
            to = lax.rem(row + d, n_row)
            points.append(remote(
                x_ref.at[pl.ds(pl.multiple_of(to * rows + c * step, step), step), :],
                xbuf.at[row, pl.ds(c * step, step), :],
                x_send.at[d - 1, c], x_recv.at[d - 1, c], {"row": to},
            ))

    def score(o0, o1):
        for o2 in range(1, d2):
            gathered[(o0, o1, o2)].wait_recv()
        base = pl.multiple_of(base_of(o0, o1, -1) * size, pair)
        whole = panels[pl.ds(base, pair), :].astype(F32)
        norms[pl.ds(base, pair), :] = jnp.broadcast_to(
            jnp.sum(whole * whole, axis=1, keepdims=True), (pair, 128)
        )
        left = panels[pl.ds(base, pair), pl.ds(pl.multiple_of(row * feats, feats), feats)]

        @pl.loop(0, rows // LANES)
        def _(c):
            lane = pl.multiple_of(c * LANES, LANES)
            logits[pl.ds(base, pair), pl.ds(lane, LANES)] = lax.dot_general(
                left, xbuf[row, pl.ds(lane, LANES), :], (((1,), (1,)), ((), ())),
                preferred_element_type=F32,
            )

    own_x.wait()
    own_panel.wait()
    order = [(0, 0)] + [(0, o1) for o1 in range(1, d1)] + [(o0, 0) for o0 in range(1, d0)]
    order += [(o0, o1) for o0 in range(1, d0) for o1 in range(1, d1)]
    before = None
    for o0, o1 in order:
        if (o0, o1) != (0, 0):
            gathered[(o0, o1, 0)].wait_recv()
            if o1 == 0:
                for hop in range(1, d1):
                    gather((o0, 0, 0), 1, hop)
            for hop in range(1, d2):
                gather((o0, o1, 0), 2, hop)
        if before is not None:
            score(*before)
        before = (o0, o1)
    score(*before)
    for copy in points:
        copy.wait_recv()

    top[...] = jnp.full(top.shape, -1e30, F32)
    total[...] = jnp.zeros(total.shape, F32)
    scale = 1.0 / (jnp.full((1, LANES), heat_ref[0], F32) * math.sqrt(width))
    tiles = rows // LANES

    @pl.loop(0, n_blk // d2 * tiles)
    def _(t):
        g = lax.div(t, tiles)
        lane = pl.multiple_of(lax.rem(t, tiles) * LANES, LANES)
        base = pl.multiple_of(g * pair, pair)
        dots = logits[pl.ds(base, pair), pl.ds(lane, LANES)]
        for d in range(1, n_row):
            other = lax.rem(row + d, n_row)
            dots += lax.dot_general(
                panels[pl.ds(base, pair), pl.ds(pl.multiple_of(other * feats, feats), feats)],
                xbuf[other, pl.ds(lane, LANES), :], (((1,), (1,)), ((), ())),
                preferred_element_type=F32,
            )
        for j in range(d2):
            value = (2.0 * dots[j * size:(j + 1) * size] - norms[pl.ds(base + j * size, size), :1]) * scale
            value = value + bias_ref[g * d2 + j, :, pl.ds(lane, LANES)]
            logits[pl.ds(base + j * size, size), pl.ds(lane, LANES)] = value
            best = jnp.max(value.reshape(size // 8, 8, LANES), axis=0)
            top[:, pl.ds(lane, LANES)] = jnp.maximum(top[:, pl.ds(lane, LANES)], best)

    peak = jnp.max(top[...], axis=0, keepdims=True)
    top[...] = jnp.broadcast_to(peak, top.shape)

    @pl.loop(0, n_blk)
    def _(g):
        base = pl.multiple_of(g * size, size)
        value = jnp.exp(logits[pl.ds(base, size), :] - top[0:1, :])
        logits[pl.ds(base, size), :] = value
        total[...] += jnp.sum(value.reshape(size // 8, 8, rows), axis=0)

    summed = jnp.sum(total[...], axis=0, keepdims=True)
    lse_ref[...] = top[0:1, :] + jnp.log(summed)
    total[...] = jnp.broadcast_to(1.0 / summed, total.shape)

    masses = []
    sent_c = {}
    sent_b = {}
    sent_a = {}

    def weigh(o0, o1):
        owner = base_of(o0, o1, 1)
        base = pl.multiple_of(owner * size, pair)
        k = o0 * d1 + o1

        weights[...] = (logits[pl.ds(base, pair), :] * total[0:1, :]).astype(BF16)

        @pl.loop(0, n_row)
        def _(s):
            part[k, :, pl.ds(pl.multiple_of(s * feats, feats), feats)] = jnp.dot(
                weights[...], xbuf[s], preferred_element_type=F32
            ).astype(BF16)

        for o2 in range(1, d2):
            j = lax.rem(i2 + o2, d2)
            sent_c[(o0, o1, o2)] = remote(
                part.at[k, pl.ds(pl.multiple_of(j * size, size), size), :],
                in_c.at[k, o2 - 1], c_send.at[k, o2 - 1], c_recv.at[k, o2 - 1],
                {"blk": at(0, 0, o2, 1)},
            )
        mass = lax.dot_general(
            jnp.ones((8, rows), BF16), weights[...], (((1,), (1,)), ((), ())),
            preferred_element_type=F32,
        )
        for j in range(d2):
            mass_out[owner + j] = mass[:, j * size:(j + 1) * size]
        for o2 in range(d2):
            if (o0, o1, o2) != (0, 0, 0):
                to = at(o0, o1, o2, 1)
                masses.append(remote(
                    mass_out.at[to], mass_in.at[blk],
                    m_send.at[o0, o1, o2], m_recv.at[o0, o1, o2], {"blk": to},
                ))

    def chip_sum(o0, o1):
        k = o0 * d1 + o1
        value = part[k, pl.ds(pl.multiple_of(i2 * size, size), size), :].astype(F32)
        for o2 in range(1, d2):
            sent_c[(o0, o1, o2)].wait_recv()
            value = value + in_c[k, o2 - 1].astype(F32)
        if o1 > 0:
            send_b[o0, o1 - 1] = value.astype(BF16)
            sent_b[(o0, o1)] = remote(
                send_b.at[o0, o1 - 1], in_b.at[o0, o1 - 1],
                b_send.at[o0, o1 - 1], b_recv.at[o0, o1 - 1], {"blk": at(0, o1, 0, 1)},
            )
            return None
        for hop in range(1, d1):
            sent_b[(o0, hop)].wait_recv()
            value = value + in_b[o0, hop - 1].astype(F32)
        if o0 > 0:
            send_a[o0 - 1] = value.astype(BF16)
            sent_a[o0] = remote(
                send_a.at[o0 - 1], in_a.at[o0 - 1],
                a_send.at[o0 - 1], a_recv.at[o0 - 1], {"blk": at(o0, 0, 0, 1)},
            )
            return None
        return value

    outer = list(range(1, d0)) + [0]
    order = [(o0, o1) for o1 in range(1, d1) for o0 in outer] + [(o0, 0) for o0 in outer]
    before = None
    for o0, o1 in order:
        weigh(o0, o1)
        if before is not None:
            chip_sum(*before)
        before = (o0, o1)
    value = chip_sum(*before)

    mass_in[blk] = mass_out[blk]
    for copy in masses:
        copy.wait_recv()
    mass = mass_in[0]
    for g in range(1, n_blk):
        mass = mass + mass_in[g]
    column = jnp.broadcast_to(mass[0:1, :], (size, size)).T[:, 0:1]
    value = value + panels[pl.ds(pl.multiple_of(blk * size, size), size), :].astype(F32)
    for o0 in range(1, d0):
        sent_a[o0].wait_recv()
        value = value + in_a[o0 - 1].astype(F32)
    out_ref[...] = (value / (column + 1.0)).astype(BF16)
    for group in (gathered, sent_c, sent_b, sent_a):
        for copy in group.values():
            copy.wait_send()
    for copy in points + masses:
        copy.wait_send()


def shards(n_blk, n_row, coarse, fine, candidates, heat):
    inner = 2 if n_blk < 32 else 4
    dims = (n_blk // (inner * inner), inner, inner)
    d0, d1, d2 = dims
    blocks = candidates.shape[0]
    size, width = fine.shape
    rows = coarse.shape[0] // n_row
    feats = coarse.shape[1]
    ids = jnp.arange(n_blk, dtype=jnp.int32)
    named = jnp.any(candidates[None, :, :] == ids[:, None, None], axis=2)
    bias = jnp.where(named, 0.0, -1e30).astype(F32)
    bias = jnp.repeat(bias, rows // blocks, axis=1).reshape(n_blk, 1, rows)
    vmem = pl.BlockSpec(memory_space=pltpu.VMEM)
    hbm = pl.BlockSpec(memory_space=pl.ANY)
    groups = d0 * d1
    chunks = 4
    dma = pltpu.SemaphoreType.DMA
    new, log_norm = pl.pallas_call(
        functools.partial(kernel, dims, n_row),
        out_shape=(
            jax.ShapeDtypeStruct((size, width), BF16),
            jax.ShapeDtypeStruct((1, rows), F32),
        ),
        in_specs=[hbm, hbm, vmem, pl.BlockSpec(memory_space=pltpu.SMEM)],
        out_specs=(vmem, vmem),
        scratch_shapes=[
            pltpu.VMEM((n_row, rows, feats), BF16),
            pltpu.VMEM((n_blk * size, width), BF16),
            pltpu.VMEM((n_blk * size, rows), F32),
            pltpu.VMEM((n_blk * size, 128), F32),
            pltpu.VMEM((8, rows), F32),
            pltpu.VMEM((8, rows), F32),
            pltpu.VMEM((d2 * size, rows), BF16),
            pltpu.VMEM((groups, d2 * size, width), BF16),
            pltpu.VMEM((groups, d2 - 1, size, width), BF16),
            pltpu.VMEM((d0, d1 - 1, size, width), BF16),
            pltpu.VMEM((d0, d1 - 1, size, width), BF16),
            pltpu.VMEM((d0 - 1, size, width), BF16),
            pltpu.VMEM((d0 - 1, size, width), BF16),
            pltpu.VMEM((n_blk, 8, size), F32),
            pltpu.VMEM((n_blk, 8, size), F32),
            dma((n_row - 1, chunks)), dma((n_row - 1, chunks)),
            dma(dims), dma(dims),
            dma((groups, d2 - 1)), dma((groups, d2 - 1)),
            dma((d0, d1 - 1)), dma((d0, d1 - 1)),
            dma((d0 - 1,)), dma((d0 - 1,)),
            dma(dims), dma(dims),
            dma((2,)),
        ],
        compiler_params=pltpu.CompilerParams(
            collective_id=0, has_side_effects=True, vmem_limit_bytes=60 << 20
        ),
        cost_estimate=pl.CostEstimate(
            flops=4 * rows * n_blk * size * width, bytes_accessed=8 << 20,
            transcendentals=rows * n_blk * size,
        ),
    )(coarse, fine, bias, heat)
    return new, log_norm.reshape(rows)


def solution(mesh):
    return jax.shard_map(
        functools.partial(shards, mesh.shape["blk"], mesh.shape["row"]),
        mesh=mesh,
        in_specs=(P("blk", "row"), P(("blk", "row"), None), P(("blk", "row"), None), P()),
        out_specs=(P(("blk", "row"), None), P(("blk", "row"))),
        check_vma=False,
    )
```

time: 198 us -> 92.9 us (0.47)
  the two profiles are of different devices: /device:TPU:0 before, /device:TPU:8 now
where the time goes in v2:
time: 92.9 us; the launch traced here: 92.7 us
  Pallas kernels  86.9 us (94%)
  local copies, waits for them, and re-layouts  3.72 us (4%)
  between operations  1.29 us (1%)
    pallas_call x1, Pallas kernels, shards(): pl.pallas_call(functools.partial(kernel, dims, n_row), out_shape=(jax.Sha...  86.9 us
    unnamed x2, local copies, waits for them, and re-layouts  2.94 us

profile of v2, /device:TPU:8, one launch (start us, length us, event | category | flops | bytes accessed | tf_op | source)
XLA Modules:
  0.0 92.7 jit_solution(8550017644324340980)
XLA Ops:
  1.3 0.8 fusion
  2.1 0.1 copy.6
  2.1 0.7 broadcast_in_dim.15
  2.9 86.9 %shard_map.59 = (bf16[128,1024]{1,0:T(8,128)(2,1)}, f32[1,1024]{1,0:T(1,128)}) custom-call(bf16[2048,512]{1,0:T(8,128)(2,1)} %x_ref.1, bf16[128,1024]{1,0:T(8,128)(2,1)} %fine_ref.1, f32[16,1,1024]{2,1,0:T(1,128)} %bitcast.2, f32[1]{0:T(128)S(6)} %copy.9.heat_ref), custom_call_target="tpu_custom_call" | custom-call | flops 8589934592 | bytes 8388608 | tf_op jit(solution)/shard_map/pallas_call | solution.py:296
  89.7 1.7 %copy.10 = bf16[128,1024]{1,0:T(8,128)(2,1)} copy(bf16[128,1024]{1,0:T(8,128)(2,1)} %get-tuple-element.8) | data formatting | bytes 524288
  91.4 1.3 %copy.11 = f32[1024]{0:T(1024)} copy(f32[1024]{0:T(1024)} %bitcast.3) | data formatting | bytes 8192
  (1 shorter events, 0.0 us)

commit v3 on v2

v3 whole, which is shorter than its diff:
```python
import functools
import math

import jax
import jax.numpy as jnp
from jax import lax
from jax.experimental import pallas as pl
from jax.experimental.pallas import tpu as pltpu
from jax.sharding import PartitionSpec as P

MESH = pl.DeviceIdType.MESH
F32 = jnp.float32
BF16 = jnp.bfloat16
LANES = 256
DEPTH = 3


def kernel(
    dims, n_row, x_ref, fine_ref, named_ref, heat_ref, out_ref, lse_ref,
    xbuf, panels, logits, norms, bias, top, peaks, total, weights, part, in_c, send_b, in_b,
    send_a, in_a, acc, mass_out, mass_in,
    x_send, x_recv, z_send, z_recv, gx_send, gx_recv, gc_send, gc_recv, c_send, c_recv,
    b_send, b_recv, a_send, a_recv, m_send, m_recv, own_sem,
):
    d0, d1, d2 = dims
    n_blk = d0 * d1 * d2
    row = lax.axis_index("row")
    blk = lax.axis_index("blk")
    i2 = lax.rem(blk, d2)
    i1 = lax.rem(lax.div(blk, d2), d1)
    i0 = lax.div(blk, d1 * d2)
    size = fine_ref.shape[0]
    width = fine_ref.shape[1]
    rows = xbuf.shape[1]
    feats = xbuf.shape[2]
    pair = d2 * size
    half = size // 2
    chunks = x_send.shape[1]
    step = rows // chunks
    blocks, names = named_ref.shape

    def near(i, o, d):
        return lax.rem(i + o + d, d)

    def index(a, b, c):
        return (a * d1 + b) * d2 + c

    def panel(owner):
        return panels.at[pl.ds(pl.multiple_of(owner * size, size), size), :]

    def remote(src, dst, send, recv, to, axis="blk"):
        return pltpu.make_async_remote_copy(
            src_ref=src, dst_ref=dst, send_sem=send, recv_sem=recv,
            device_id={axis: to}, device_id_type=MESH,
        )

    barrier = pltpu.get_barrier_semaphore()
    for d in range(1, n_row):
        pl.semaphore_signal(
            barrier, inc=1, device_id={"row": near(row, d, n_row)}, device_id_type=MESH
        )
    for d in range(1, n_blk):
        pl.semaphore_signal(
            barrier, inc=1, device_id={"blk": near(blk, d, n_blk)}, device_id_type=MESH
        )
    own_x = pltpu.make_async_copy(
        x_ref.at[pl.ds(pl.multiple_of(row * rows, rows), rows), :], xbuf.at[row], own_sem.at[0]
    )
    own_x.start()
    own_panel = pltpu.make_async_copy(fine_ref, panel(blk), own_sem.at[1])
    own_panel.start()
    pl.semaphore_wait(barrier, n_row - 1 + n_blk - 1)

    def z_copy(way, k, own=False):
        sign = 1 - 2 * way
        owner = index(i0 - sign * (k - 1), i1, i2)
        return remote(
            fine_ref if own else panel(owner), panel(owner),
            z_send.at[way, k - 1], z_recv.at[way, k - 1], index(i0 + sign, i1, i2),
        )

    def x_copy(a, o1, own=False):
        owner = index(a, i1, i2)
        return remote(
            fine_ref if own else panel(owner), panel(owner),
            gx_send.at[a, o1 - 1], gx_recv.at[a, o1 - 1], index(i0, near(i1, o1, d1), i2),
        )

    def c_copy(a, o1, o2, own=False):
        owner = index(a, near(i1, -o1, d1), i2)
        return remote(
            fine_ref if own else panel(owner), panel(owner),
            gc_send.at[a, o1, o2 - 1], gc_recv.at[a, o1, o2 - 1],
            index(i0, i1, near(i2, o2, d2)),
        )

    def inside(i):
        return (i >= 0) & (i < d0)

    for o1 in range(1, d1):
        x_copy(i0, o1, True).start()
    for way in range(2):
        @pl.when(inside(i0 + 1 - 2 * way))
        def _():
            z_copy(way, 1, True).start()
    for o2 in range(1, d2):
        c_copy(i0, 0, o2, True).start()
    points = []
    for c in range(chunks):
        for d in range(1, n_row):
            to = near(row, d, n_row)
            points.append(remote(
                x_ref.at[pl.ds(pl.multiple_of(to * rows + c * step, step), step), :],
                xbuf.at[row, pl.ds(c * step, step), :],
                x_send.at[d - 1, c], x_recv.at[d - 1, c], to, "row",
            ))
            points[-1].start()

    @pl.loop(0, n_blk)
    def _(g):
        for b in range(blocks):
            hit = named_ref[b, 0] == g
            for j in range(1, names):
                hit = hit | (named_ref[b, j] == g)
            bias[g, :, b * (rows // blocks):(b + 1) * (rows // blocks)] = jnp.full(
                (1, rows // blocks), jnp.where(hit, 0.0, -1e30), F32
            )

    def score(a, o1):
        for o2 in range(1, d2):
            c_copy(a, o1, o2).wait_recv()
        base = pl.multiple_of(index(a, near(i1, -o1, d1), 0) * size, pair)
        whole = panels[pl.ds(base, pair), :].astype(F32)
        norms[pl.ds(base, pair), :] = jnp.broadcast_to(
            jnp.sum(whole * whole, axis=1, keepdims=True), (pair, 128)
        )
        left = panels[pl.ds(base, pair), pl.ds(pl.multiple_of(row * feats, feats), feats)]

        @pl.loop(0, rows // LANES)
        def _(c):
            lane = pl.multiple_of(c * LANES, LANES)
            logits[pl.ds(base, pair), pl.ds(lane, LANES)] = lax.dot_general(
                left, xbuf[row, pl.ds(lane, LANES), :], (((1,), (1,)), ((), ())),
                preferred_element_type=F32,
            )

    def z_event(way, k):
        sign = 1 - 2 * way

        @pl.when(inside(i0 - sign * k))
        def _():
            z_copy(way, k).wait_recv()
            if k < d0 - 1:
                @pl.when(inside(i0 + sign))
                def _():
                    z_copy(way, k + 1).start()
            a = i0 - sign * k
            for o1 in range(1, d1):
                x_copy(a, o1).start()
            for o2 in range(1, d2):
                c_copy(a, 0, o2).start()

    def x_event(a):
        for o1 in range(1, d1):
            x_copy(a, o1).wait_recv()
            for o2 in range(1, d2):
                c_copy(a, o1, o2).start()
        for o1 in range(d1):
            score(a, o1)

    own_x.wait()
    own_panel.wait()
    for k in range(1, d0 + 1):
        if k < d0:
            for way in range(2):
                z_event(way, k)
        if k == 1:
            x_event(i0)
        else:
            for way in range(2):
                a = i0 - (1 - 2 * way) * (k - 1)

                @pl.when(inside(a))
                def _():
                    x_event(a)
    for copy in points:
        copy.wait_recv()

    top[...] = jnp.full(top.shape, -1e30, F32)
    total[...] = jnp.zeros(total.shape, F32)
    scale = 1.0 / (jnp.full((1, LANES), heat_ref[0], F32) * math.sqrt(width))
    tiles = rows // LANES

    @pl.loop(0, n_blk // d2 * tiles)
    def _(t):
        g = lax.div(t, tiles)
        lane = pl.multiple_of(lax.rem(t, tiles) * LANES, LANES)
        lanes = pl.ds(lane, LANES)
        base = pl.multiple_of(g * pair, pair)
        dots = logits[pl.ds(base, pair), lanes]
        for d in range(1, n_row):
            other = near(row, d, n_row)
            dots += lax.dot_general(
                panels[pl.ds(base, pair), pl.ds(pl.multiple_of(other * feats, feats), feats)],
                xbuf[other, lanes, :], (((1,), (1,)), ((), ())),
                preferred_element_type=F32,
            )
        values = []
        old = top[0:1, lanes]
        best = jnp.broadcast_to(old, (8, LANES))
        for j in range(d2):
            norm = norms[pl.ds(base + j * size, size), :1]
            value = (2.0 * dots[j * size:(j + 1) * size] - norm) * scale
            values.append(value + bias[g * d2 + j, :, lanes])
            best = jnp.maximum(best, jnp.max(values[j].reshape(size // 8, 8, LANES), axis=0))
        best = jnp.max(best, axis=0, keepdims=True)
        added = total[:, lanes] * jnp.exp(old - best)
        for j in range(d2):
            value = jnp.exp(values[j] - best)
            logits[pl.ds(base + j * size, size), lanes] = value
            added = added + jnp.sum(value.reshape(size // 8, 8, LANES), axis=0)
        total[:, lanes] = added
        top[:, lanes] = jnp.broadcast_to(best, (8, LANES))
        peaks[g, :, lanes] = best

    summed = jnp.sum(total[...], axis=0, keepdims=True)
    lse_ref[...] = top[0:1, :] + jnp.log(summed)
    total[...] = jnp.broadcast_to(1.0 / summed, total.shape)

    def target(k):
        value = 0
        for z in range(d0):
            far = sorted(range(d0), key=lambda t: (-abs(t - z), t if z >= d0 // 2 else -t))
            value = jnp.where(i0 == z, far[k], value)
        return value

    targets = [target(k) for k in range(d0)]

    def c_sum(k, o1, o2):
        j = near(i2, o2, d2)
        return remote(
            part.at[k * d1 + o1, pl.ds(pl.multiple_of(j * size, size), size), :],
            in_c.at[k * d1 + o1, o2 - 1], c_send.at[k * d1 + o1, o2 - 1],
            c_recv.at[k * d1 + o1, o2 - 1], index(i0, i1, j),
        )

    def b_sum(k, o1, h):
        spot = pl.ds(h * half, half)
        return remote(
            send_b.at[k, o1 - 1, spot, :], in_b.at[k, o1 - 1, spot, :],
            b_send.at[k, o1 - 1, h], b_recv.at[k, o1 - 1, h],
            index(i0, near(i1, o1, d1), i2),
        )

    def a_sum(k, h, way, goal):
        spot = pl.ds(h * half, half)
        return remote(
            send_a.at[min(k, d0 - 2), spot, :], in_a.at[way, goal, spot, :],
            a_send.at[min(k, d0 - 2), h], a_recv.at[way, goal, h],
            index(near(i0, 1 - 2 * way, d0), i1, i2),
        )

    def m_sum(o0, o1, o2):
        to = index(near(i0, o0, d0), near(i1, o1, d1), near(i2, o2, d2))
        return remote(
            mass_out.at[to], mass_in.at[blk], m_send.at[o0, o1, o2], m_recv.at[o0, o1, o2], to
        )

    def weigh(k, o1):
        owner = index(targets[k], near(i1, o1, d1), 0)
        base = pl.multiple_of(owner * size, pair)
        factor = jnp.exp(peaks[lax.div(owner, d2)] - top[0:1, :]) * total[0:1, :]
        weights[...] = (logits[pl.ds(base, pair), :] * factor).astype(BF16)

        @pl.loop(0, n_row)
        def _(s):
            part[k * d1 + o1, :, pl.ds(pl.multiple_of(s * feats, feats), feats)] = jnp.dot(
                weights[...], xbuf[s], preferred_element_type=F32
            ).astype(BF16)

        for o2 in range(1, d2):
            c_sum(k, o1, o2).start()
        mass = lax.dot_general(
            jnp.ones((8, rows), BF16), weights[...], (((1,), (1,)), ((), ())),
            preferred_element_type=F32,
        )
        for j in range(d2):
            mass_out[owner + j] = mass[:, j * size:(j + 1) * size]

    def chip_sum(k, o1, begin, count):
        start = pl.multiple_of(i2 * size + begin, half)
        value = part[k * d1 + o1, pl.ds(start, count), :].astype(F32)
        for o2 in range(1, d2):
            value = value + in_c[k * d1 + o1, o2 - 1, begin:begin + count, :].astype(F32)
        return value

    def ready(k):
        for o1 in range(1, d1):
            for o2 in range(1, d2):
                c_sum(k, o1, o2).wait_recv()
            send_b[k, o1 - 1] = chip_sum(k, o1, 0, size).astype(BF16)

    halves = [(k, h) for k in range(d0) for h in range(2)]

    def pass_on(position):
        if position < len(halves):
            k, h = halves[position]
            for o1 in range(1, d1):
                b_sum(k, o1, h).start()

    started = 0
    for k in range(d0):
        for o1 in range(1, d1):
            weigh(k, o1)
        if k > 0:
            ready(k - 1)
            while started < min(DEPTH, 2 * k):
                pass_on(started)
                started += 1
    weigh(0, 0)
    ready(d0 - 1)
    while started < min(DEPTH, 2 * d0):
        pass_on(started)
        started += 1

    for position, (k, h) in enumerate(halves):
        if h == 0 and k < d0 - 1:
            weigh(k + 1, 0)
            if k == d0 - 2:
                for o0 in range(d0):
                    for o1 in range(d1):
                        for o2 in range(d2):
                            if (o0, o1, o2) != (0, 0, 0):
                                m_sum(o0, o1, o2).start()
        for o1 in range(1, d1):
            b_sum(k, o1, h).wait_recv()
        pass_on(position + DEPTH)
        if h == 0:
            for o2 in range(1, d2):
                c_sum(k, 0, o2).wait_recv()
        value = chip_sum(k, 0, h * half, half)
        for o1 in range(1, d1):
            value = value + in_b[k, o1 - 1, h * half:(h + 1) * half, :].astype(F32)
        spot = pl.ds(h * half, half)
        acc[spot, :] = value
        goal = targets[k]
        if k < d0 - 1:
            way = jnp.where(goal > i0, 0, 1)

            @pl.when(inside(i0 - 1 + 2 * way))
            def _():
                a_sum(k, h, way, goal).wait_recv()
                acc[spot, :] += in_a[way, goal, spot, :].astype(F32)

            send_a[k, spot, :] = acc[spot, :].astype(BF16)
            a_sum(k, h, way, goal).start()

    mass_in[blk] = mass_out[blk]
    mass = None
    for o0 in range(d0):
        for o1 in range(d1):
            for o2 in range(d2):
                if (o0, o1, o2) != (0, 0, 0):
                    m_sum(o0, o1, o2).wait_recv()
    mass = mass_in[0]
    for g in range(1, n_blk):
        mass = mass + mass_in[g]
    column = jnp.broadcast_to(mass[0:1, :], (size, size)).T[:, 0:1] + 1.0
    acc[...] += panels[pl.ds(pl.multiple_of(blk * size, size), size), :].astype(F32)
    for h in range(2):
        spot = pl.ds(h * half, half)
        for way in range(2):
            @pl.when(inside(i0 - 1 + 2 * way))
            def _():
                a_sum(d0 - 1, h, way, i0).wait_recv()
                acc[spot, :] += in_a[way, i0, spot, :].astype(F32)
        out_ref[spot, :] = (acc[spot, :] / column[h * half:(h + 1) * half]).astype(BF16)

    for copy in points:
        copy.wait_send()
    for way in range(2):
        sign = 1 - 2 * way
        for k in range(1, d0):
            @pl.when(inside(i0 + sign) & inside(i0 - sign * (k - 1)))
            def _():
                z_copy(way, k).wait_send()
    for a in range(d0):
        for o1 in range(1, d1):
            x_copy(a, o1).wait_send()
        for o1 in range(d1):
            for o2 in range(1, d2):
                c_copy(a, o1, o2).wait_send()
                c_sum(a, o1, o2).wait_send()
        for h in range(2):
            for o1 in range(1, d1):
                b_sum(a, o1, h).wait_send()
            if a < d0 - 1:
                a_sum(a, h, 0, i0).wait_send()
    for o0 in range(d0):
        for o1 in range(d1):
            for o2 in range(d2):
                if (o0, o1, o2) != (0, 0, 0):
                    m_sum(o0, o1, o2).wait_send()


def shards(n_blk, n_row, coarse, fine, candidates, heat):
    inner = 2 if n_blk < 32 else 4
    dims = (n_blk // (inner * inner), inner, inner)
    d0, d1, d2 = dims
    size, width = fine.shape
    rows = coarse.shape[0] // n_row
    feats = coarse.shape[1]
    vmem = pl.BlockSpec(memory_space=pltpu.VMEM)
    hbm = pl.BlockSpec(memory_space=pl.ANY)
    smem = pl.BlockSpec(memory_space=pltpu.SMEM)
    groups = d0 * d1
    chunks = 4
    dma = pltpu.SemaphoreType.DMA
    new, log_norm = pl.pallas_call(
        functools.partial(kernel, dims, n_row),
        out_shape=(
            jax.ShapeDtypeStruct((size, width), BF16),
            jax.ShapeDtypeStruct((1, rows), F32),
        ),
        in_specs=[hbm, hbm, smem, smem],
        out_specs=(vmem, vmem),
        scratch_shapes=[
            pltpu.VMEM((n_row, rows, feats), BF16),
            pltpu.VMEM((n_blk * size, width), BF16),
            pltpu.VMEM((n_blk * size, rows), F32),
            pltpu.VMEM((n_blk * size, 128), F32),
            pltpu.VMEM((n_blk, 1, rows), F32),
            pltpu.VMEM((8, rows), F32),
            pltpu.VMEM((groups, 1, rows), F32),
            pltpu.VMEM((8, rows), F32),
            pltpu.VMEM((d2 * size, rows), BF16),
            pltpu.VMEM((groups, d2 * size, width), BF16),
            pltpu.VMEM((groups, d2 - 1, size, width), BF16),
            pltpu.VMEM((d0, d1 - 1, size, width), BF16),
            pltpu.VMEM((d0, d1 - 1, size, width), BF16),
            pltpu.VMEM((d0 - 1, size, width), BF16),
            pltpu.VMEM((2, d0, size, width), BF16),
            pltpu.VMEM((size, width), F32),
            pltpu.VMEM((n_blk, 8, size), F32),
            pltpu.VMEM((n_blk, 8, size), F32),
            dma((n_row - 1, chunks)), dma((n_row - 1, chunks)),
            dma((2, d0 - 1)), dma((2, d0 - 1)),
            dma((d0, d1 - 1)), dma((d0, d1 - 1)),
            dma((d0, d1, d2 - 1)), dma((d0, d1, d2 - 1)),
            dma((groups, d2 - 1)), dma((groups, d2 - 1)),
            dma((d0, d1 - 1, 2)), dma((d0, d1 - 1, 2)),
            dma((d0 - 1, 2)), dma((2, d0, 2)),
            dma(dims), dma(dims),
            dma((2,)),
        ],
        compiler_params=pltpu.CompilerParams(
            collective_id=0, has_side_effects=True, vmem_limit_bytes=60 << 20
        ),
        cost_estimate=pl.CostEstimate(
            flops=4 * rows * n_blk * size * width, bytes_accessed=8 << 20,
            transcendentals=rows * n_blk * size,
        ),
    )(coarse, fine, candidates, heat)
    return new, log_norm.reshape(rows)


def solution(mesh):
    return jax.shard_map(
        functools.partial(shards, mesh.shape["blk"], mesh.shape["row"]),
        mesh=mesh,
        in_specs=(P("blk", "row"), P(("blk", "row"), None), P(("blk", "row"), None), P()),
        out_specs=(P(("blk", "row"), None), P(("blk", "row"))),
        check_vma=False,
    )
```

time: 92.9 us -> 82.8 us (0.89)
  the two profiles are of different devices: /device:TPU:8 before, /device:TPU:0 now
where the time goes in v3:
time: 82.8 us; the launch traced here: 82.5 us
  Pallas kernels  78.3 us (95%)
  local copies, waits for them, and re-layouts  2.95 us (4%)
  between operations  1.29 us (2%)
    pallas_call x1, Pallas kernels, shards(): pl.pallas_call(functools.partial(kernel, dims, n_row), out_shape=(jax.Sha...  78.3 us
    unnamed x2, local copies, waits for them, and re-layouts  2.95 us

profile of v3, /device:TPU:0, one launch (start us, length us, event | category | flops | bytes accessed | tf_op | source)
XLA Modules:
  0.0 82.5 jit_solution(15752645050733147935)
XLA Ops:
  1.3 78.3 %shard_map.59 = (bf16[128,1024]{1,0:T(8,128)(2,1)}, f32[1,1024]{1,0:T(1,128)}) custom-call(bf16[2048,512]{1,0:T(8,128)(2,1)} %x_ref.1, bf16[128,1024]{1,0:T(8,128)(2,1)} %fine_ref.1, s32[8,8]{1,0:T(8,128)} %named_ref.1, f32[1]{0:T(128)S(6)} %copy.8.heat_ref), custom_call_target="tpu_custom_call" | custom-call | flops 8589934592 | bytes 8388608 | tf_op jit(solution)/shard_map/pallas_call | solution.py:419
  79.6 1.7 %copy.9 = bf16[128,1024]{1,0:T(8,128)(2,1)} copy(bf16[128,1024]{1,0:T(8,128)(2,1)} %get-tuple-element.8) | data formatting | bytes 524288
  81.3 1.3 %copy.10 = f32[1024]{0:T(1024)} copy(f32[1024]{0:T(1024)} %bitcast.1) | data formatting | bytes 8192

commit v4 on v3

--- a/solution.py
+++ b/solution.py
@@ -13,6 +13,7 @@
 BF16 = jnp.bfloat16
 LANES = 256
 DEPTH = 3
+SPAN = 4
 
 
 def kernel(
@@ -126,6 +127,10 @@
                 (1, rows // blocks), jnp.where(hit, 0.0, -1e30), F32
             )
 
+    scale = 1.0 / (jnp.full((1, LANES), heat_ref[0], F32) * math.sqrt(width))
+    top[...] = jnp.full(top.shape, -1e30, F32)
+    total[...] = jnp.zeros(total.shape, F32)
+
     def score(a, o1):
         for o2 in range(1, d2):
             c_copy(a, o1, o2).wait_recv()
@@ -133,7 +138,7 @@
         whole = panels[pl.ds(base, pair), :].astype(F32)
         norms[pl.ds(base, pair), :] = jnp.broadcast_to(
             jnp.sum(whole * whole, axis=1, keepdims=True), (pair, 128)
-        )
+        ) * scale[:, :128]
         left = panels[pl.ds(base, pair), pl.ds(pl.multiple_of(row * feats, feats), feats)]
 
         @pl.loop(0, rows // LANES)
@@ -168,54 +173,31 @@
         for o1 in range(d1):
             score(a, o1)
 
-    own_x.wait()
-    own_panel.wait()
-    for k in range(1, d0 + 1):
-        if k < d0:
-            for way in range(2):
-                z_event(way, k)
-        if k == 1:
-            x_event(i0)
-        else:
-            for way in range(2):
-                a = i0 - (1 - 2 * way) * (k - 1)
-
-                @pl.when(inside(a))
-                def _():
-                    x_event(a)
-    for copy in points:
-        copy.wait_recv()
-
-    top[...] = jnp.full(top.shape, -1e30, F32)
-    total[...] = jnp.zeros(total.shape, F32)
-    scale = 1.0 / (jnp.full((1, LANES), heat_ref[0], F32) * math.sqrt(width))
-    tiles = rows // LANES
-
-    @pl.loop(0, n_blk // d2 * tiles)
-    def _(t):
-        g = lax.div(t, tiles)
-        lane = pl.multiple_of(lax.rem(t, tiles) * LANES, LANES)
-        lanes = pl.ds(lane, LANES)
-        base = pl.multiple_of(g * pair, pair)
-        dots = logits[pl.ds(base, pair), lanes]
+    spans = n_blk // SPAN
+
+    def fuse(g, c):
+        lanes = pl.ds(c * LANES, LANES)
+        base = pl.multiple_of(g * (SPAN * size), SPAN * size)
+        tile = pl.ds(base, SPAN * size)
+        dots = logits[tile, lanes]
         for d in range(1, n_row):
             other = near(row, d, n_row)
             dots += lax.dot_general(
-                panels[pl.ds(base, pair), pl.ds(pl.multiple_of(other * feats, feats), feats)],
+                panels[tile, pl.ds(pl.multiple_of(other * feats, feats), feats)],
                 xbuf[other, lanes, :], (((1,), (1,)), ((), ())),
                 preferred_element_type=F32,
             )
         values = []
         old = top[0:1, lanes]
         best = jnp.broadcast_to(old, (8, LANES))
-        for j in range(d2):
+        for j in range(SPAN):
             norm = norms[pl.ds(base + j * size, size), :1]
-            value = (2.0 * dots[j * size:(j + 1) * size] - norm) * scale
-            values.append(value + bias[g * d2 + j, :, lanes])
+            value = dots[j * size:(j + 1) * size] * (2.0 * scale) - norm
+            values.append(value + bias[g * SPAN + j, :, lanes])
             best = jnp.maximum(best, jnp.max(values[j].reshape(size // 8, 8, LANES), axis=0))
         best = jnp.max(best, axis=0, keepdims=True)
         added = total[:, lanes] * jnp.exp(old - best)
-        for j in range(d2):
+        for j in range(SPAN):
             value = jnp.exp(values[j] - best)
             logits[pl.ds(base + j * size, size), lanes] = value
             added = added + jnp.sum(value.reshape(size // 8, 8, LANES), axis=0)
@@ -223,6 +205,38 @@
         top[:, lanes] = jnp.broadcast_to(best, (8, LANES))
         peaks[g, :, lanes] = best
 
+    own_x.wait()
+    own_panel.wait()
+    late = jnp.where(i0 < d0 // 2, d0 - 1, 0)
+    for k in range(1, d0):
+        for way in range(2):
+            z_event(way, k)
+        if k == 1:
+            x_event(i0)
+        else:
+            for way in range(2):
+                a = i0 - (1 - 2 * way) * (k - 1)
+
+                @pl.when(inside(a) & (a != late))
+                def _():
+                    x_event(a)
+
+    each = d1 * d2 // SPAN
+    first = jnp.where(late == 0, each, 0)
+    for c in range(chunks):
+        for copy in points[c * (n_row - 1):(c + 1) * (n_row - 1)]:
+            copy.wait_recv()
+
+        @pl.loop(0, spans - each)
+        def _(g):
+            fuse(first + g, c)
+
+    x_event(late)
+    for c in range(chunks):
+        @pl.loop(0, each)
+        def _(g):
+            fuse(late * each + g, c)
+
     summed = jnp.sum(total[...], axis=0, keepdims=True)
     lse_ref[...] = top[0:1, :] + jnp.log(summed)
     total[...] = jnp.broadcast_to(1.0 / summed, total.shape)
@@ -269,7 +283,7 @@
     def weigh(k, o1):
         owner = index(targets[k], near(i1, o1, d1), 0)
         base = pl.multiple_of(owner * size, pair)
-        factor = jnp.exp(peaks[lax.div(owner, d2)] - top[0:1, :]) * total[0:1, :]
+        factor = jnp.exp(peaks[lax.div(owner, SPAN)] - top[0:1, :]) * total[0:1, :]
         weights[...] = (logits[pl.ds(base, pair), :] * factor).astype(BF16)
 
         @pl.loop(0, n_row)
@@ -414,7 +428,7 @@
     hbm = pl.BlockSpec(memory_space=pl.ANY)
     smem = pl.BlockSpec(memory_space=pltpu.SMEM)
     groups = d0 * d1
-    chunks = 4
+    chunks = rows // LANES
     dma = pltpu.SemaphoreType.DMA
     new, log_norm = pl.pallas_call(
         functools.partial(kernel, dims, n_row),
@@ -431,7 +445,7 @@
             pltpu.VMEM((n_blk * size, 128), F32),
             pltpu.VMEM((n_blk, 1, rows), F32),
             pltpu.VMEM((8, rows), F32),
-            pltpu.VMEM((groups, 1, rows), F32),
+            pltpu.VMEM((n_blk // SPAN, 1, rows), F32),
             pltpu.VMEM((8, rows), F32),
             pltpu.VMEM((d2 * size, rows), BF16),
             pltpu.VMEM((groups, d2 * size, width), BF16),

time: 82.8 us -> 75.8 us (0.915)
  Pallas kernels: 78.3 us -> 71.4 us
    pallas_call x1, Pallas kernels: 78.3 us -> 71.4 us  [shards(): pl.pallas_call(functools.partial(kernel, dims, n_row), out_shape=(jax.Sha...]
where the time goes in v4:
time: 75.8 us; the launch traced here: 75.6 us
  Pallas kernels  71.4 us (94%)
  local copies, waits for them, and re-layouts  2.95 us (4%)
  between operations  1.29 us (2%)
    pallas_call x1, Pallas kernels, shards(): pl.pallas_call(functools.partial(kernel, dims, n_row), out_shape=(jax.Sha...  71.4 us
    unnamed x2, local copies, waits for them, and re-layouts  2.95 us

profile of v4, /device:TPU:0, one launch (start us, length us, event | category | flops | bytes accessed | tf_op | source)
XLA Modules:
  0.0 75.6 jit_solution(11938491623975084217)
XLA Ops:
  1.3 71.4 %shard_map.59 = (bf16[128,1024]{1,0:T(8,128)(2,1)}, f32[1,1024]{1,0:T(1,128)}) custom-call(bf16[2048,512]{1,0:T(8,128)(2,1)} %x_ref.1, bf16[128,1024]{1,0:T(8,128)(2,1)} %fine_ref.1, s32[8,8]{1,0:T(8,128)} %named_ref.1, f32[1]{0:T(128)S(6)} %copy.8.heat_ref), custom_call_target="tpu_custom_call" | custom-call | flops 8589934592 | bytes 8388608 | tf_op jit(solution)/shard_map/pallas_call | solution.py:433
  72.6 1.7 %copy.9 = bf16[128,1024]{1,0:T(8,128)(2,1)} copy(bf16[128,1024]{1,0:T(8,128)(2,1)} %get-tuple-element.8) | data formatting | bytes 524288
  74.3 1.3 %copy.10 = f32[1024]{0:T(1024)} copy(f32[1024]{0:T(1024)} %bitcast.1) | data formatting | bytes 8192

commit v5 on v4

--- a/solution.py
+++ b/solution.py
@@ -115,7 +115,13 @@
                 xbuf.at[row, pl.ds(c * step, step), :],
                 x_send.at[d - 1, c], x_recv.at[d - 1, c], to, "row",
             ))
-            points[-1].start()
+
+    def send_points(c):
+        for copy in points[c * (n_row - 1):(c + 1) * (n_row - 1)]:
+            copy.start()
+
+    for c in range(min(2, chunks)):
+        send_points(c)
 
     @pl.loop(0, n_blk)
     def _(g):
@@ -131,7 +137,7 @@
     top[...] = jnp.full(top.shape, -1e30, F32)
     total[...] = jnp.zeros(total.shape, F32)
 
-    def score(a, o1):
+    def measure(a, o1):
         for o2 in range(1, d2):
             c_copy(a, o1, o2).wait_recv()
         base = pl.multiple_of(index(a, near(i1, -o1, d1), 0) * size, pair)
@@ -139,6 +145,10 @@
         norms[pl.ds(base, pair), :] = jnp.broadcast_to(
             jnp.sum(whole * whole, axis=1, keepdims=True), (pair, 128)
         ) * scale[:, :128]
+        return base
+
+    def score(a, o1):
+        base = measure(a, o1)
         left = panels[pl.ds(base, pair), pl.ds(pl.multiple_of(row * feats, feats), feats)]
 
         @pl.loop(0, rows // LANES)
@@ -165,45 +175,50 @@
             for o2 in range(1, d2):
                 c_copy(a, 0, o2).start()
 
-    def x_event(a):
+    def x_arrival(a):
         for o1 in range(1, d1):
             x_copy(a, o1).wait_recv()
             for o2 in range(1, d2):
                 c_copy(a, o1, o2).start()
+
+    def x_event(a):
+        x_arrival(a)
         for o1 in range(d1):
             score(a, o1)
 
-    spans = n_blk // SPAN
-
-    def fuse(g, c):
+    joint = max(1, min(d1, SPAN // d2))
+
+    def fuse(g, c, count, full=False):
         lanes = pl.ds(c * LANES, LANES)
-        base = pl.multiple_of(g * (SPAN * size), SPAN * size)
-        tile = pl.ds(base, SPAN * size)
-        dots = logits[tile, lanes]
-        for d in range(1, n_row):
+        base = pl.multiple_of(g * pair, pair)
+        tile = pl.ds(base, count * pair)
+        dots = None if full else logits[tile, lanes]
+        for d in range(0 if full else 1, n_row):
             other = near(row, d, n_row)
-            dots += lax.dot_general(
+            term = lax.dot_general(
                 panels[tile, pl.ds(pl.multiple_of(other * feats, feats), feats)],
                 xbuf[other, lanes, :], (((1,), (1,)), ((), ())),
                 preferred_element_type=F32,
             )
+            dots = term if dots is None else dots + term
         values = []
         old = top[0:1, lanes]
         best = jnp.broadcast_to(old, (8, LANES))
-        for j in range(SPAN):
+        for j in range(count * d2):
             norm = norms[pl.ds(base + j * size, size), :1]
             value = dots[j * size:(j + 1) * size] * (2.0 * scale) - norm
-            values.append(value + bias[g * SPAN + j, :, lanes])
+            values.append(value + bias[g * d2 + j, :, lanes])
             best = jnp.maximum(best, jnp.max(values[j].reshape(size // 8, 8, LANES), axis=0))
         best = jnp.max(best, axis=0, keepdims=True)
         added = total[:, lanes] * jnp.exp(old - best)
-        for j in range(SPAN):
+        for j in range(count * d2):
             value = jnp.exp(values[j] - best)
             logits[pl.ds(base + j * size, size), lanes] = value
             added = added + jnp.sum(value.reshape(size // 8, 8, LANES), axis=0)
         total[:, lanes] = added
         top[:, lanes] = jnp.broadcast_to(best, (8, LANES))
-        peaks[g, :, lanes] = best
+        for j in range(count):
+            peaks[g + j, :, lanes] = best
 
     own_x.wait()
     own_panel.wait()
@@ -220,22 +235,30 @@
                 @pl.when(inside(a) & (a != late))
                 def _():
                     x_event(a)
-
-    each = d1 * d2 // SPAN
-    first = jnp.where(late == 0, each, 0)
+        if k + 1 < chunks:
+            send_points(k + 1)
+    for c in range(max(2, d0 + 1), chunks):
+        send_points(c)
+    score(late, 0)
+
+    each = d1 // joint
+    first = jnp.where(late == 0, d1, 0)
     for c in range(chunks):
+        if c == chunks - 1:
+            x_arrival(late)
         for copy in points[c * (n_row - 1):(c + 1) * (n_row - 1)]:
             copy.wait_recv()
-
-        @pl.loop(0, spans - each)
+        fuse(late * d1 + i1, c, 1)
+
+        @pl.loop(0, (d0 - 1) * each)
         def _(g):
-            fuse(first + g, c)
-
-    x_event(late)
-    for c in range(chunks):
-        @pl.loop(0, each)
-        def _(g):
-            fuse(late * each + g, c)
+            fuse(first + g * joint, c, joint)
+
+    for o1 in range(1, d1):
+        measure(late, o1)
+        g = late * d1 + near(i1, -o1, d1)
+        for c in range(chunks):
+            fuse(g, c, 1, True)
 
     summed = jnp.sum(total[...], axis=0, keepdims=True)
     lse_ref[...] = top[0:1, :] + jnp.log(summed)
@@ -283,7 +306,7 @@
     def weigh(k, o1):
         owner = index(targets[k], near(i1, o1, d1), 0)
         base = pl.multiple_of(owner * size, pair)
-        factor = jnp.exp(peaks[lax.div(owner, SPAN)] - top[0:1, :]) * total[0:1, :]
+        factor = jnp.exp(peaks[lax.div(owner, d2)] - top[0:1, :]) * total[0:1, :]
         weights[...] = (logits[pl.ds(base, pair), :] * factor).astype(BF16)
 
         @pl.loop(0, n_row)
@@ -445,7 +468,7 @@
             pltpu.VMEM((n_blk * size, 128), F32),
             pltpu.VMEM((n_blk, 1, rows), F32),
             pltpu.VMEM((8, rows), F32),
-            pltpu.VMEM((n_blk // SPAN, 1, rows), F32),
+            pltpu.VMEM((groups, 1, rows), F32),
             pltpu.VMEM((8, rows), F32),
             pltpu.VMEM((d2 * size, rows), BF16),
             pltpu.VMEM((groups, d2 * size, width), BF16),

time: 75.8 us -> 76.4 us (level)
  no operation moved by 1% of the time
where the time goes in v5:
time: 76.4 us; the launch traced here: 76.2 us
  Pallas kernels  72 us (94%)
  local copies, waits for them, and re-layouts  2.95 us (4%)
  between operations  1.29 us (2%)
    pallas_call x1, Pallas kernels, shards(): pl.pallas_call(functools.partial(kernel, dims, n_row), out_shape=(jax.Sha...  72 us
    unnamed x2, local copies, waits for them, and re-layouts  2.95 us

profile of v5, /device:TPU:0, one launch (start us, length us, event | category | flops | bytes accessed | tf_op | source)
XLA Modules:
  0.0 76.2 jit_solution(1204557006696169654)
XLA Ops:
  1.3 72.0 %shard_map.59 = (bf16[128,1024]{1,0:T(8,128)(2,1)}, f32[1,1024]{1,0:T(1,128)}) custom-call(bf16[2048,512]{1,0:T(8,128)(2,1)} %x_ref.1, bf16[128,1024]{1,0:T(8,128)(2,1)} %fine_ref.1, s32[8,8]{1,0:T(8,128)} %named_ref.1, f32[1]{0:T(128)S(6)} %copy.8.heat_ref), custom_call_target="tpu_custom_call" | custom-call | flops 8589934592 | bytes 8388608 | tf_op jit(solution)/shard_map/pallas_call | solution.py:456
  73.2 1.7 %copy.9 = bf16[128,1024]{1,0:T(8,128)(2,1)} copy(bf16[128,1024]{1,0:T(8,128)(2,1)} %get-tuple-element.8) | data formatting | bytes 524288
  74.9 1.3 %copy.10 = f32[1024]{0:T(1024)} copy(f32[1024]{0:T(1024)} %bitcast.1) | data formatting | bytes 8192

commit v6 on v5

--- a/solution.py
+++ b/solution.py
@@ -19,8 +19,8 @@
 def kernel(
     dims, n_row, x_ref, fine_ref, named_ref, heat_ref, out_ref, lse_ref,
     xbuf, panels, logits, norms, bias, top, peaks, total, weights, part, in_c, send_b, in_b,
-    send_a, in_a, acc, mass_out, mass_in,
-    x_send, x_recv, z_send, z_recv, gx_send, gx_recv, gc_send, gc_recv, c_send, c_recv,
+    send_a, in_a, send_w, in_w, edge, acc, mass_out, mass_in,
+    x_send, x_recv, z_send, z_recv, w_send, w_recv, s_send, s_recv, gx_send, gx_recv, gc_send, gc_recv, c_send, c_recv,
     b_send, b_recv, a_send, a_recv, m_send, m_recv, own_sem,
 ):
     d0, d1, d2 = dims
@@ -72,19 +72,32 @@
     own_panel.start()
     pl.semaphore_wait(barrier, n_row - 1 + n_blk - 1)
 
-    def z_copy(way, k, own=False):
+    cut = size - size // 8
+    pieces = (pl.ds(0, half), pl.ds(half, cut - half), pl.ds(cut, size - cut))
+
+    def z_copy(way, k, h, own=False):
         sign = 1 - 2 * way
-        owner = index(i0 - sign * (k - 1), i1, i2)
-        return remote(
-            fine_ref if own else panel(owner), panel(owner),
-            z_send.at[way, k - 1], z_recv.at[way, k - 1], index(i0 + sign, i1, i2),
-        )
-
-    def x_copy(a, o1, own=False):
-        owner = index(a, i1, i2)
-        return remote(
-            fine_ref if own else panel(owner), panel(owner),
-            gx_send.at[a, o1 - 1], gx_recv.at[a, o1 - 1], index(i0, near(i1, o1, d1), i2),
+        spot = pl.ds(h * half, half)
+        there = panel(index(i0 - sign * (k - 1), i1, i2)).at[spot, :]
+        return remote(
+            fine_ref.at[spot, :] if own else there, there,
+            z_send.at[way, k - 1, h], z_recv.at[way, k - 1, h], index(i0 + sign, i1, i2),
+        )
+
+    def w_copy(way, k, o1):
+        sign = 1 - 2 * way
+        there = panel(index(i0 - sign * (k - 1), near(i1, -o1, d1), i2)).at[pieces[2], :]
+        return remote(
+            there, there, w_send.at[way, k - 1, o1 - 1], w_recv.at[way, k - 1, o1 - 1],
+            index(i0 + sign, i1, i2),
+        )
+
+    def x_copy(a, o1, p, own=False):
+        there = panel(index(a, i1, i2)).at[pieces[p], :]
+        return remote(
+            fine_ref.at[pieces[p], :] if own else there, there,
+            gx_send.at[a, o1 - 1, p], gx_recv.at[a, o1 - 1, p],
+            index(i0, near(i1, o1, d1), i2),
         )
 
     def c_copy(a, o1, o2, own=False):
@@ -98,12 +111,14 @@
     def inside(i):
         return (i >= 0) & (i < d0)
 
-    for o1 in range(1, d1):
-        x_copy(i0, o1, True).start()
+    for p in (2, 0, 1):
+        for o1 in range(1, d1):
+            x_copy(i0, o1, p, True).start()
     for way in range(2):
         @pl.when(inside(i0 + 1 - 2 * way))
         def _():
-            z_copy(way, 1, True).start()
+            for h in range(2):
+                z_copy(way, 1, h, True).start()
     for o2 in range(1, d2):
         c_copy(i0, 0, o2, True).start()
     points = []
@@ -120,8 +135,15 @@
         for copy in points[c * (n_row - 1):(c + 1) * (n_row - 1)]:
             copy.start()
 
-    for c in range(min(2, chunks)):
+    for c in range(chunks):
         send_points(c)
+    for o1 in range(1, d1):
+        x_copy(i0, o1, 2).wait_recv()
+    for way in range(2):
+        @pl.when(inside(i0 + 1 - 2 * way))
+        def _():
+            for o1 in range(1, d1):
+                w_copy(way, 1, o1).start()
 
     @pl.loop(0, n_blk)
     def _(g):
@@ -159,25 +181,40 @@
                 preferred_element_type=F32,
             )
 
-    def z_event(way, k):
+    def z_event(way, k, h):
         sign = 1 - 2 * way
-
-        @pl.when(inside(i0 - sign * k))
+        a = i0 - sign * k
+
+        @pl.when(inside(a))
         def _():
-            z_copy(way, k).wait_recv()
+            z_copy(way, k, h).wait_recv()
             if k < d0 - 1:
                 @pl.when(inside(i0 + sign))
                 def _():
-                    z_copy(way, k + 1).start()
-            a = i0 - sign * k
-            for o1 in range(1, d1):
-                x_copy(a, o1).start()
-            for o2 in range(1, d2):
-                c_copy(a, 0, o2).start()
+                    z_copy(way, k + 1, h).start()
+            for o1 in range(1, d1):
+                x_copy(a, o1, h).start()
+            if h == 1:
+                for o2 in range(1, d2):
+                    c_copy(a, 0, o2).start()
+
+    def w_event(way, k):
+        sign = 1 - 2 * way
+
+        @pl.when(inside(i0 - sign * k))
+        def _():
+            for o1 in range(1, d1):
+                w_copy(way, k, o1).wait_recv()
+            if k < d0 - 1:
+                @pl.when(inside(i0 + sign))
+                def _():
+                    for o1 in range(1, d1):
+                        w_copy(way, k + 1, o1).start()
 
     def x_arrival(a):
         for o1 in range(1, d1):
-            x_copy(a, o1).wait_recv()
+            for p in range(2):
+                x_copy(a, o1, p).wait_recv()
             for o2 in range(1, d2):
                 c_copy(a, o1, o2).start()
 
@@ -224,8 +261,11 @@
     own_panel.wait()
     late = jnp.where(i0 < d0 // 2, d0 - 1, 0)
     for k in range(1, d0):
+        for h in range(2):
+            for way in range(2):
+                z_event(way, k, h)
         for way in range(2):
-            z_event(way, k)
+            w_event(way, k)
         if k == 1:
             x_event(i0)
         else:
@@ -235,10 +275,6 @@
                 @pl.when(inside(a) & (a != late))
                 def _():
                     x_event(a)
-        if k + 1 < chunks:
-            send_points(k + 1)
-    for c in range(max(2, d0 + 1), chunks):
-        send_points(c)
     score(late, 0)
 
     each = d1 // joint
@@ -282,7 +318,7 @@
         )
 
     def b_sum(k, o1, h):
-        spot = pl.ds(h * half, half)
+        spot = pl.ds(h * half, half if h == 0 or k == d0 - 1 else cut - half)
         return remote(
             send_b.at[k, o1 - 1, spot, :], in_b.at[k, o1 - 1, spot, :],
             b_send.at[k, o1 - 1, h], b_recv.at[k, o1 - 1, h],
@@ -296,6 +332,30 @@
             a_send.at[min(k, d0 - 2), h], a_recv.at[way, goal, h],
             index(near(i0, 1 - 2 * way, d0), i1, i2),
         )
+
+    def w_sum(k, o1, way, goal):
+        return remote(
+            send_w.at[min(k, d0 - 2), o1 - 1], in_w.at[way, goal, o1 - 1],
+            s_send.at[min(k, d0 - 2), o1 - 1], s_recv.at[way, goal, o1 - 1],
+            index(near(i0, 1 - 2 * way, d0), i1, i2),
+        )
+
+    def around(k):
+        goal = targets[k]
+        last = k == d0 - 1
+        for o1 in range(1, d1):
+            edge[...] = send_b[k, o1 - 1, cut:, :].astype(F32)
+            for way in (0, 1) if last else (jnp.where(goal > i0, 0, 1),):
+                @pl.when(inside(i0 - 1 + 2 * way))
+                def _():
+                    w_sum(k, o1, way, goal).wait_recv()
+                    edge[...] += in_w[way, goal, o1 - 1].astype(F32)
+
+            if last:
+                send_b[k, o1 - 1, cut:, :] = edge[...].astype(BF16)
+            else:
+                send_w[k, o1 - 1] = edge[...].astype(BF16)
+                w_sum(k, o1, way, goal).start()
 
     def m_sum(o0, o1, o2):
         to = index(near(i0, o0, d0), near(i1, o1, d1), near(i2, o2, d2))
@@ -371,15 +431,25 @@
                                 m_sum(o0, o1, o2).start()
         for o1 in range(1, d1):
             b_sum(k, o1, h).wait_recv()
-        pass_on(position + DEPTH)
+        if position + DEPTH < len(halves) - 1:
+            pass_on(position + DEPTH)
+        if h == 0 and k < d0 - 1:
+            around(k)
+        if position + DEPTH == len(halves) - 1:
+            around(d0 - 1)
+            pass_on(position + DEPTH)
         if h == 0:
             for o2 in range(1, d2):
                 c_sum(k, 0, o2).wait_recv()
         value = chip_sum(k, 0, h * half, half)
         for o1 in range(1, d1):
-            value = value + in_b[k, o1 - 1, h * half:(h + 1) * half, :].astype(F32)
+            if h == 0 or k == d0 - 1:
+                value = value + in_b[k, o1 - 1, h * half:(h + 1) * half, :].astype(F32)
         spot = pl.ds(h * half, half)
         acc[spot, :] = value
+        if h == 1 and k < d0 - 1:
+            for o1 in range(1, d1):
+                acc[half:cut, :] += in_b[k, o1 - 1, half:cut, :].astype(F32)
         goal = targets[k]
         if k < d0 - 1:
             way = jnp.where(goal > i0, 0, 1)
@@ -420,10 +490,16 @@
         for k in range(1, d0):
             @pl.when(inside(i0 + sign) & inside(i0 - sign * (k - 1)))
             def _():
-                z_copy(way, k).wait_send()
+                for h in range(2):
+                    z_copy(way, k, h).wait_send()
+                for o1 in range(1, d1):
+                    w_copy(way, k, o1).wait_send()
+    for o1 in range(1, d1):
+        x_copy(i0, o1, 2).wait_send()
     for a in range(d0):
         for o1 in range(1, d1):
-            x_copy(a, o1).wait_send()
+            for p in range(2):
+                x_copy(a, o1, p).wait_send()
         for o1 in range(d1):
             for o2 in range(1, d2):
                 c_copy(a, o1, o2).wait_send()
@@ -433,6 +509,9 @@
                 b_sum(a, o1, h).wait_send()
             if a < d0 - 1:
                 a_sum(a, h, 0, i0).wait_send()
+        if a < d0 - 1:
+            for o1 in range(1, d1):
+                w_sum(a, o1, 0, i0).wait_send()
     for o0 in range(d0):
         for o1 in range(d1):
             for o2 in range(d2):
@@ -477,12 +556,17 @@
             pltpu.VMEM((d0, d1 - 1, size, width), BF16),
             pltpu.VMEM((d0 - 1, size, width), BF16),
             pltpu.VMEM((2, d0, size, width), BF16),
+            pltpu.VMEM((d0 - 1, d1 - 1, size // 8, width), BF16),
+            pltpu.VMEM((2, d0, d1 - 1, size // 8, width), BF16),
+            pltpu.VMEM((size // 8, width), F32),
             pltpu.VMEM((size, width), F32),
             pltpu.VMEM((n_blk, 8, size), F32),
             pltpu.VMEM((n_blk, 8, size), F32),
             dma((n_row - 1, chunks)), dma((n_row - 1, chunks)),
-            dma((2, d0 - 1)), dma((2, d0 - 1)),
-            dma((d0, d1 - 1)), dma((d0, d1 - 1)),
+            dma((2, d0 - 1, 2)), dma((2, d0 - 1, 2)),
+            dma((2, d0 - 1, d1 - 1)), dma((2, d0 - 1, d1 - 1)),
+            dma((d0 - 1, d1 - 1)), dma((2, d0, d1 - 1)),
+            dma((d0, d1 - 1, 3)), dma((d0, d1 - 1, 3)),
             dma((d0, d1, d2 - 1)), dma((d0, d1, d2 - 1)),
             dma((groups, d2 - 1)), dma((groups, d2 - 1)),
             dma((d0, d1 - 1, 2)), dma((d0, d1 - 1, 2)),

time: 76.4 us -> 78.3 us (1.025)
  Pallas kernels: 72 us -> 73.8 us
    pallas_call x1, Pallas kernels: 72 us -> 73.8 us  [shards(): pl.pallas_call(functools.partial(kernel, dims, n_row), out_shape=(jax.Sha...]
where the time goes in v6:
time: 78.3 us; the launch traced here: 78 us
  Pallas kernels  73.8 us (94%)
  local copies, waits for them, and re-layouts  2.95 us (4%)
  between operations  1.29 us (2%)
    pallas_call x1, Pallas kernels, shards(): pl.pallas_call(functools.partial(kernel, dims, n_row), out_shape=(jax.Sha...  73.8 us
    unnamed x2, local copies, waits for them, and re-layouts  2.95 us

profile of v6, /device:TPU:0, one launch (start us, length us, event | category | flops | bytes accessed | tf_op | source)
XLA Modules:
  0.0 78.0 jit_solution(16322780278212076492)
XLA Ops:
  1.3 73.8 %shard_map.59 = (bf16[128,1024]{1,0:T(8,128)(2,1)}, f32[1,1024]{1,0:T(1,128)}) custom-call(bf16[2048,512]{1,0:T(8,128)(2,1)} %x_ref.1, bf16[128,1024]{1,0:T(8,128)(2,1)} %fine_ref.1, s32[8,8]{1,0:T(8,128)} %named_ref.1, f32[1]{0:T(128)S(6)} %copy.8.heat_ref), custom_call_target="tpu_custom_call" | custom-call | flops 8589934592 | bytes 8388608 | tf_op jit(solution)/shard_map/pallas_call | solution.py:535
  75.1 1.7 %copy.9 = bf16[128,1024]{1,0:T(8,128)(2,1)} copy(bf16[128,1024]{1,0:T(8,128)(2,1)} %get-tuple-element.8) | data formatting | bytes 524288
  76.7 1.3 %copy.10 = f32[1024]{0:T(1024)} copy(f32[1024]{0:T(1024)} %bitcast.1) | data formatting | bytes 8192

commit v7 on v5

--- a/solution.py
+++ b/solution.py
@@ -12,7 +12,7 @@
 F32 = jnp.float32
 BF16 = jnp.bfloat16
 LANES = 256
-DEPTH = 3
+DEPTH = 4
 SPAN = 4
 
 
@@ -120,7 +120,7 @@
         for copy in points[c * (n_row - 1):(c + 1) * (n_row - 1)]:
             copy.start()
 
-    for c in range(min(2, chunks)):
+    for c in range(chunks):
         send_points(c)
 
     @pl.loop(0, n_blk)
@@ -235,10 +235,6 @@
                 @pl.when(inside(a) & (a != late))
                 def _():
                     x_event(a)
-        if k + 1 < chunks:
-            send_points(k + 1)
-    for c in range(max(2, d0 + 1), chunks):
-        send_points(c)
     score(late, 0)
 
     each = d1 // joint
@@ -349,11 +345,12 @@
     for k in range(d0):
         for o1 in range(1, d1):
             weigh(k, o1)
-        if k > 0:
-            ready(k - 1)
-            while started < min(DEPTH, 2 * k):
-                pass_on(started)
-                started += 1
+        done = max(k, 1)
+        if k != 1:
+            ready(done - 1)
+        while started < min(DEPTH, 2 * done):
+            pass_on(started)
+            started += 1
     weigh(0, 0)
     ready(d0 - 1)
     while started < min(DEPTH, 2 * d0):
@@ -361,14 +358,6 @@
         started += 1
 
     for position, (k, h) in enumerate(halves):
-        if h == 0 and k < d0 - 1:
-            weigh(k + 1, 0)
-            if k == d0 - 2:
-                for o0 in range(d0):
-                    for o1 in range(d1):
-                        for o2 in range(d2):
-                            if (o0, o1, o2) != (0, 0, 0):
-                                m_sum(o0, o1, o2).start()
         for o1 in range(1, d1):
             b_sum(k, o1, h).wait_recv()
         pass_on(position + DEPTH)
@@ -391,6 +380,14 @@
 
             send_a[k, spot, :] = acc[spot, :].astype(BF16)
             a_sum(k, h, way, goal).start()
+            if h == 0:
+                weigh(k + 1, 0)
+                if k == d0 - 2:
+                    for o0 in range(d0):
+                        for o1 in range(d1):
+                            for o2 in range(d2):
+                                if (o0, o1, o2) != (0, 0, 0):
+                                    m_sum(o0, o1, o2).start()
 
     mass_in[blk] = mass_out[blk]
     mass = None

time: 76.4 us -> 76.4 us (level)
  no operation moved by 1% of the time
where the time goes in v7:
time: 76.4 us; the launch traced here: 76.2 us
  Pallas kernels  72 us (94%)
  local copies, waits for them, and re-layouts  2.95 us (4%)
  between operations  1.29 us (2%)
    pallas_call x1, Pallas kernels, shards(): pl.pallas_call(functools.partial(kernel, dims, n_row), out_shape=(jax.Sha...  72 us
    unnamed x2, local copies, waits for them, and re-layouts  2.95 us

profile of v7, /device:TPU:0, one launch (start us, length us, event | category | flops | bytes accessed | tf_op | source)
XLA Modules:
  0.0 76.2 jit_solution(15377212558657760575)
XLA Ops:
  1.3 72.0 %shard_map.59 = (bf16[128,1024]{1,0:T(8,128)(2,1)}, f32[1,1024]{1,0:T(1,128)}) custom-call(bf16[2048,512]{1,0:T(8,128)(2,1)} %x_ref.1, bf16[128,1024]{1,0:T(8,128)(2,1)} %fine_ref.1, s32[8,8]{1,0:T(8,128)} %named_ref.1, f32[1]{0:T(128)S(6)} %copy.8.heat_ref), custom_call_target="tpu_custom_call" | custom-call | flops 8589934592 | bytes 8388608 | tf_op jit(solution)/shard_map/pallas_call | solution.py:453
  73.2 1.7 %copy.9 = bf16[128,1024]{1,0:T(8,128)(2,1)} copy(bf16[128,1024]{1,0:T(8,128)(2,1)} %get-tuple-element.8) | data formatting | bytes 524288
  74.9 1.3 %copy.10 = f32[1024]{0:T(1024)} copy(f32[1024]{0:T(1024)} %bitcast.1) | data formatting | bytes 8192

commit v8 on v7

--- a/solution.py
+++ b/solution.py
@@ -12,7 +12,6 @@
 F32 = jnp.float32
 BF16 = jnp.bfloat16
 LANES = 256
-DEPTH = 4
 SPAN = 4
 
 
@@ -88,7 +87,7 @@
         )
 
     def c_copy(a, o1, o2, own=False):
-        owner = index(a, near(i1, -o1, d1), i2)
+        owner = index(a, near(i1, d1 - o1, d1), i2)
         return remote(
             fine_ref if own else panel(owner), panel(owner),
             gc_send.at[a, o1, o2 - 1], gc_recv.at[a, o1, o2 - 1],
@@ -106,22 +105,17 @@
             z_copy(way, 1, True).start()
     for o2 in range(1, d2):
         c_copy(i0, 0, o2, True).start()
-    points = []
+    def x_points(d, c):
+        to = near(row, d, n_row)
+        return remote(
+            x_ref.at[pl.ds(pl.multiple_of(to * rows + c * step, step), step), :],
+            xbuf.at[row, pl.ds(pl.multiple_of(c * step, step), step), :],
+            x_send.at[d - 1, c], x_recv.at[d - 1, c], to, "row",
+        )
+
     for c in range(chunks):
         for d in range(1, n_row):
-            to = near(row, d, n_row)
-            points.append(remote(
-                x_ref.at[pl.ds(pl.multiple_of(to * rows + c * step, step), step), :],
-                xbuf.at[row, pl.ds(c * step, step), :],
-                x_send.at[d - 1, c], x_recv.at[d - 1, c], to, "row",
-            ))
-
-    def send_points(c):
-        for copy in points[c * (n_row - 1):(c + 1) * (n_row - 1)]:
-            copy.start()
-
-    for c in range(chunks):
-        send_points(c)
+            x_points(d, c).start()
 
     @pl.loop(0, n_blk)
     def _(g):
@@ -140,7 +134,7 @@
     def measure(a, o1):
         for o2 in range(1, d2):
             c_copy(a, o1, o2).wait_recv()
-        base = pl.multiple_of(index(a, near(i1, -o1, d1), 0) * size, pair)
+        base = pl.multiple_of(index(a, near(i1, d1 - o1, d1), 0) * size, pair)
         whole = panels[pl.ds(base, pair), :].astype(F32)
         norms[pl.ds(base, pair), :] = jnp.broadcast_to(
             jnp.sum(whole * whole, axis=1, keepdims=True), (pair, 128)
@@ -165,10 +159,10 @@
         @pl.when(inside(i0 - sign * k))
         def _():
             z_copy(way, k).wait_recv()
-            if k < d0 - 1:
-                @pl.when(inside(i0 + sign))
-                def _():
-                    z_copy(way, k + 1).start()
+            @pl.when((k < d0 - 1) & inside(i0 + sign))
+            def _():
+                z_copy(way, k + 1).start()
+
             a = i0 - sign * k
             for o1 in range(1, d1):
                 x_copy(a, o1).start()
@@ -183,13 +177,15 @@
 
     def x_event(a):
         x_arrival(a)
-        for o1 in range(d1):
+
+        @pl.loop(0, d1)
+        def _(o1):
             score(a, o1)
 
     joint = max(1, min(d1, SPAN // d2))
 
     def fuse(g, c, count, full=False):
-        lanes = pl.ds(c * LANES, LANES)
+        lanes = pl.ds(pl.multiple_of(c * LANES, LANES), LANES)
         base = pl.multiple_of(g * pair, pair)
         tile = pl.ds(base, count * pair)
         dots = None if full else logits[tile, lanes]
@@ -223,27 +219,30 @@
     own_x.wait()
     own_panel.wait()
     late = jnp.where(i0 < d0 // 2, d0 - 1, 0)
-    for k in range(1, d0):
+
+    @pl.loop(1, d0)
+    def _(k):
         for way in range(2):
             z_event(way, k)
-        if k == 1:
-            x_event(i0)
-        else:
-            for way in range(2):
-                a = i0 - (1 - 2 * way) * (k - 1)
-
-                @pl.when(inside(a) & (a != late))
-                def _():
-                    x_event(a)
+        for way in range(2):
+            a = i0 - (1 - 2 * way) * (k - 1)
+
+            @pl.when(inside(a) & (a != late) & ((k > 1) | (way == 0)))
+            def _():
+                x_event(a)
+
     score(late, 0)
 
     each = d1 // joint
     first = jnp.where(late == 0, d1, 0)
-    for c in range(chunks):
-        if c == chunks - 1:
+    @pl.loop(0, chunks)
+    def _(c):
+        @pl.when(c == chunks - 1)
+        def _():
             x_arrival(late)
-        for copy in points[c * (n_row - 1):(c + 1) * (n_row - 1)]:
-            copy.wait_recv()
+
+        for d in range(1, n_row):
+            x_points(d, c).wait_recv()
         fuse(late * d1 + i1, c, 1)
 
         @pl.loop(0, (d0 - 1) * each)
@@ -253,7 +252,9 @@
     for o1 in range(1, d1):
         measure(late, o1)
         g = late * d1 + near(i1, -o1, d1)
-        for c in range(chunks):
+
+        @pl.loop(0, chunks)
+        def _(c):
             fuse(g, c, 1, True)
 
     summed = jnp.sum(total[...], axis=0, keepdims=True)
@@ -300,7 +301,10 @@
         )
 
     def weigh(k, o1):
-        owner = index(targets[k], near(i1, o1, d1), 0)
+        goal = targets[0]
+        for other in range(1, d0):
+            goal = jnp.where(k == other, targets[other], goal)
+        owner = index(goal, near(i1, o1, d1), 0)
         base = pl.multiple_of(owner * size, pair)
         factor = jnp.exp(peaks[lax.div(owner, d2)] - top[0:1, :]) * total[0:1, :]
         weights[...] = (logits[pl.ds(base, pair), :] * factor).astype(BF16)
@@ -327,40 +331,33 @@
             value = value + in_c[k * d1 + o1, o2 - 1, begin:begin + count, :].astype(F32)
         return value
 
-    def ready(k):
-        for o1 in range(1, d1):
-            for o2 in range(1, d2):
-                c_sum(k, o1, o2).wait_recv()
-            send_b[k, o1 - 1] = chip_sum(k, o1, 0, size).astype(BF16)
+    def ready(k, o1):
+        for o2 in range(1, d2):
+            c_sum(k, o1, o2).wait_recv()
+        send_b[k, o1 - 1] = chip_sum(k, o1, 0, size).astype(BF16)
+        for h in range(2):
+            b_sum(k, o1, h).start()
 
     halves = [(k, h) for k in range(d0) for h in range(2)]
 
-    def pass_on(position):
-        if position < len(halves):
-            k, h = halves[position]
-            for o1 in range(1, d1):
-                b_sum(k, o1, h).start()
-
-    started = 0
-    for k in range(d0):
-        for o1 in range(1, d1):
-            weigh(k, o1)
-        done = max(k, 1)
-        if k != 1:
-            ready(done - 1)
-        while started < min(DEPTH, 2 * done):
-            pass_on(started)
-            started += 1
-    weigh(0, 0)
-    ready(d0 - 1)
-    while started < min(DEPTH, 2 * d0):
-        pass_on(started)
-        started += 1
+    jobs = d0 * (d1 - 1)
+
+    def job(i):
+        return lax.div(i, d1 - 1), 1 + lax.rem(i, d1 - 1)
+
+    @pl.loop(0, jobs + 1)
+    def _(i):
+        k, o1 = job(i)
+        end = i == jobs
+        weigh(jnp.where(end, 0, k), jnp.where(end, 0, o1))
+
+        @pl.when(i > 0)
+        def _():
+            ready(*job(i - 1))
 
     for position, (k, h) in enumerate(halves):
         for o1 in range(1, d1):
             b_sum(k, o1, h).wait_recv()
-        pass_on(position + DEPTH)
         if h == 0:
             for o2 in range(1, d2):
                 c_sum(k, 0, o2).wait_recv()
@@ -410,8 +407,9 @@
                 acc[spot, :] += in_a[way, i0, spot, :].astype(F32)
         out_ref[spot, :] = (acc[spot, :] / column[h * half:(h + 1) * half]).astype(BF16)
 
-    for copy in points:
-        copy.wait_send()
+    for c in range(chunks):
+        for d in range(1, n_row):
+            x_points(d, c).wait_send()
     for way in range(2):
         sign = 1 - 2 * way
         for k in range(1, d0):

time: 76.4 us -> 76 us (level)
  no operation moved by 1% of the time
where the time goes in v8:
time: 76 us; the launch traced here: 75.7 us
  Pallas kernels  71.5 us (94%)
  local copies, waits for them, and re-layouts  2.95 us (4%)
  between operations  1.29 us (2%)
    pallas_call x1, Pallas kernels, shards(): pl.pallas_call(functools.partial(kernel, dims, n_row), out_shape=(jax.Sha...  71.5 us
    unnamed x2, local copies, waits for them, and re-layouts  2.95 us

profile of v8, /device:TPU:0, one launch (start us, length us, event | category | flops | bytes accessed | tf_op | source)
XLA Modules:
  0.0 75.7 jit_solution(8449359209818767372)
XLA Ops:
  1.3 71.5 %shard_map.59 = (bf16[128,1024]{1,0:T(8,128)(2,1)}, f32[1,1024]{1,0:T(1,128)}) custom-call(bf16[2048,512]{1,0:T(8,128)(2,1)} %x_ref.1, bf16[128,1024]{1,0:T(8,128)(2,1)} %fine_ref.1, s32[8,8]{1,0:T(8,128)} %named_ref.1, f32[1]{0:T(128)S(6)} %copy.8.heat_ref), custom_call_target="tpu_custom_call" | custom-call | flops 8589934592 | bytes 8388608 | tf_op jit(solution)/shard_map/pallas_call | solution.py:451
  72.8 1.7 %copy.9 = bf16[128,1024]{1,0:T(8,128)(2,1)} copy(bf16[128,1024]{1,0:T(8,128)(2,1)} %get-tuple-element.8) | data formatting | bytes 524288
  74.4 1.3 %copy.10 = f32[1024]{0:T(1024)} copy(f32[1024]{0:T(1024)} %bitcast.1) | data formatting | bytes 8192
